TPU v7x, 128 devices: a whole 4x4x4 slice. The times are simulated.
128 devices in a mesh: row: 4 (over y), col: 32 (over z, x, core).
Axes of the slice: x: 4, y: 4, z: 4, core: 2. Of those that a mesh axis runs over, the one named last changes fastest.
Arguments:
- tokens: bfloat16 [1536, 6144], P('row', 'col'), may hold values from -6 to 6
- norm_gain: bfloat16 [6144], P('col'), may hold values from 0.36 to 2.7
- inner_weight: bfloat16 [6144, 12288], P('row', 'col'), may hold values from -0.15625 to 0.15625
- outer_weight: bfloat16 [12288, 6144], P('col', 'row'), may hold values from -0.109375 to 0.109375
- cotangent: bfloat16 [1536, 6144], P('row', 'col'), may hold values from -6 to 6
Outputs:
- branch_out: bfloat16 [1536, 6144], P('row', 'col')
- grad_tokens: bfloat16 [1536, 6144], P('row', 'col')
- grad_gain: float32 [6144], P('col')
- grad_inner: float32 [6144, 12288], P('row', 'col')
- grad_outer: float32 [12288, 6144], P('col', 'row')
All inputs are finite; a program needn't handle non-finite values.
Results may differ from a plain program's by a relative error of at most 0.0058.
Values may be sent and summed in bfloat16 or wider, within the bound.
A program may use at most 192 MiB of HBM per device.

v0:
```python
import jax
import jax.numpy as jnp
from jax import lax
from jax.sharding import PartitionSpec as P

inv_sqrt_two = 0.7071067811865476
inv_sqrt_tau = 0.3989422804014327


def gelu_parts(hidden_pre):
    cumulative = 0.5 * (1.0 + lax.erf(hidden_pre * inv_sqrt_two))
    density = jnp.exp(-0.5 * hidden_pre * hidden_pre) * inv_sqrt_tau
    return (hidden_pre * cumulative, cumulative + hidden_pre * density)


def contract_rows(left, right):
    return lax.dot_general(
        left, right, (((0,), (0,)), ((), ())), preferred_element_type=jnp.float32
    )


def contract_cols(left, right):
    return lax.dot_general(
        left, right, (((1,), (1,)), ((), ())), preferred_element_type=jnp.float32
    )


def body(tokens, norm_gain, inner_weight, outer_weight, cotangent):
    full_rows, full_gain = (
        lax.all_gather(tokens, "col", axis=1, tiled=True),
        lax.all_gather(norm_gain, "col", axis=0, tiled=True),
    )
    values = full_rows.astype(jnp.float32)
    row_mean = jnp.mean(values, axis=1, keepdims=True)
    centred = values - row_mean
    variance = jnp.mean(centred * centred, axis=1, keepdims=True)
    inv_std = lax.rsqrt(variance + 1e-06)
    unit_rows = centred * inv_std
    gain_values = full_gain.astype(jnp.float32)
    normed = (unit_rows * gain_values).astype(jnp.bfloat16)
    inner_full = lax.all_gather(inner_weight, "row", axis=0, tiled=True)
    hidden_pre = jnp.dot(normed, inner_full, preferred_element_type=jnp.float32)
    gelu_value, gelu_slope = gelu_parts(hidden_pre)
    activated = gelu_value.astype(jnp.bfloat16)
    outer_full = lax.all_gather(outer_weight, "row", axis=1, tiled=True)
    partial_value = jnp.dot(activated, outer_full, preferred_element_type=jnp.float32)
    branch_out = lax.psum_scatter(partial_value, "col", scatter_dimension=1, tiled=True).astype(
        jnp.bfloat16
    )
    cot_full = lax.all_gather(cotangent, "col", axis=1, tiled=True)
    grad_act = contract_cols(cot_full, outer_full)
    grad_pre = (grad_act * gelu_slope).astype(jnp.bfloat16)
    grad_partial = contract_cols(grad_pre, inner_full)
    share_width = tokens.shape[1]
    offset = lax.axis_index("col") * share_width
    unit_share = lax.dynamic_slice_in_dim(unit_rows, offset, share_width, 1)
    grad_full = lax.psum(grad_partial, "col")
    grad_hat = grad_full * gain_values
    first_mean = jnp.mean(grad_hat, axis=1, keepdims=True)
    second_mean = jnp.mean(grad_hat * unit_rows, axis=1, keepdims=True)
    grad_all = inv_std * (grad_hat - first_mean - unit_rows * second_mean)
    grad_tokens = lax.dynamic_slice_in_dim(grad_all, offset, share_width, 1).astype(jnp.bfloat16)
    grad_share = lax.dynamic_slice_in_dim(grad_full, offset, share_width, 1)
    grad_gain = lax.psum(jnp.sum(grad_share * unit_share, axis=0), "row")
    grad_outer = lax.psum_scatter(
        contract_rows(activated, cot_full), "row", scatter_dimension=1, tiled=True
    )
    grad_inner = lax.psum_scatter(
        contract_rows(normed, grad_pre), "row", scatter_dimension=0, tiled=True
    )
    return (branch_out, grad_tokens, grad_gain, grad_inner, grad_outer)


def solution(mesh):
    return jax.shard_map(
        body,
        mesh=mesh,
        in_specs=(P("row", "col"), P("col"), P("row", "col"), P("col", "row"), P("row", "col")),
        out_specs=(P("row", "col"), P("row", "col"), P("col"), P("row", "col"), P("col", "row")),
        check_vma=False,
    )
```

profile of v0, /device:TPU:1, one launch (start us, length us, event | category | flops | bytes accessed | tf_op | source)
XLA Modules:
  0.0 642.2 jit_solution(6316518777295097359)
XLA Ops:
  7.2 0.0 all-gather.5.cloned.1.call-start
  7.2 0.7 all-gather.5.cloned.1.call-update
  7.9 0.0 all-gather.7.cloned.1.call-start
  7.9 0.7 all-gather.7.cloned.1.call-update
  8.6 0.0 all-gather.9.cloned.1.call-start
  8.7 0.7 all-gather.9.cloned.1.call-update
  9.4 0.0 all-gather.11.cloned.1.call-start
  9.4 0.5 all-gather.11.cloned.1.call-update
  10.0 0.0 all-reduce.3.cloned.1.call-start
  10.0 1.2 dynamic-slice
  11.9 0.9 dynamic-update-slice
  12.8 125.8 %all-reduce = bf16[6144]{0:T(1024)(128)(2,1)S(1)} all-reduce(bf16[6144]{0:T(1024)(128)(2,1)S(1)} %dynamic-update-slice), channel_id=1, replica_groups=mesh['row'=4,'col'=32] {'col'}, use_global_device_ids=true, to_apply=%add | all-reduce | flops 6144 | bytes 24576
  138.6 0.0 all-gather.5.cloned.1.call-done
  138.6 6.7 %copy.12 = bf16[384,6144]{1,0:T(8,128)(2,1)} copy(bf16[384,6144]{0,1:T(8,128)(2,1)} %all-gather.5.cloned.1.call-done) | data formatting | bytes 9437184 | tf_op jit(solution)/shard_map/all_gather | solution.py:30
  145.3 3.0 convert_reduce_fusion
  148.4 3.7 fusion.2
  152.1 0.0 all-gather.7.cloned.1.call-done
  152.1 6.1 fusion.4
  158.2 10.6 %all-gather.9.cloned.1.call-done = bf16[384,6144]{1,0:T(8,128)(2,1)} async-done(((bf16[384,1536]{1,0:T(8,128)(2,1)}), bf16[384,6144]{1,0:T(8,128)(2,1)}) %all-gather.9.cloned.1.call-update) | async-done | bytes 4718608 | tf_op jit(solution)/shard_map/all_gather | solution.py:45
  168.8 50.0 %all-gather.11.cloned.1.call-done = bf16[384,6144]{0,1:T(8,128)(2,1)} async-done(((bf16[384,192]{0,1:T(8,128)(2,1)}), bf16[384,6144]{0,1:T(8,128)(2,1)}) %all-gather.11.cloned.1.call-update) | async-done | bytes 4718608 | tf_op jit(solution)/shard_map/all_gather | solution.py:50
  218.7 0.0 copy-start
  218.7 6.6 %fusion.5 = bf16[384,384]{1,0:T(8,128)(2,1)S(1)} fusion(bf16[384,6144]{0,1:T(8,128)(2,1)} %all-gather.11.cloned.1.call-done, bf16[384,6144]{1,0:T(8,128)(2,1)} %all-gather.9.cloned.1.call-done, f32[384,384]{1,0:T(8,128)S(1)} %fusion.4), kind=kOutput, calls=%fused_computation.11 | convolution fusion | flops 1813413888 | bytes 10321920 | tf_op jit(solution)/shard_map/dot_general | solution.py:23
  225.4 0.0 copy-done
  225.4 5.2 fusion.18
  230.5 0.0 all-reduce.3.cloned.1.call-update
  230.6 0.0 reduce-scatter.4.cloned.1.call-start
  230.6 9.4 %fusion.14 = f32[384,6144]{0,1:T(8,128)} fusion(bf16[384,6144]{1,0:T(8,128)(2,1)} %all-gather.9.cloned.1.call-done, f32[384,384]{1,0:T(8,128)S(1)} %fusion.4), kind=kOutput, calls=%fused_computation.29 | convolution fusion | flops 1812676608 | bytes 14745600 | tf_op jit(solution)/shard_map/dot_general | solution.py:46
  240.0 0.0 reduce-scatter.4.cloned.1.call-update
  240.1 0.2 reduce-scatter.8.cloned.1.call-start
  240.3 8.7 %fusion.13 = f32[384,6144]{1,0:T(8,128)} fusion(bf16[384,6144]{0,1:T(8,128)(2,1)} %all-gather.11.cloned.1.call-done, f32[384,384]{1,0:T(8,128)S(1)} %fusion.4), kind=kOutput, calls=%fused_computation.28 | convolution fusion | flops 1812676608 | bytes 14745600 | tf_op jit(solution)/shard_map/dot_general | solution.py:17
  249.0 0.0 reduce-scatter.8.cloned.1.call-update
  249.0 0.0 reduce-scatter.6.cloned.1.call-start
  249.0 9.5 %fusion.3 = f32[6144,384]{1,0:T(8,128)} fusion(bf16[384,384]{1,0:T(8,128)(2,1)S(1)} %fusion.5, f32[6144]{0:T(1024)S(1)} %convert_element_type.22, bf16[384,6144]{1,0:T(8,128)(2,1)} %copy.12, f32[384]{0:T(512)S(1)} %add_rsqrt_fusion, f32[384]{0:T(512)S(1)} %broadcast_multiply_fusion.3), kind=kOutput, calls=%fused_computation.8 | convolution fusion | flops 1823735808 | bytes 14478336 | tf_op jit(solution)/shard_map/dot_general | solution.py:17
  258.5 0.0 reduce-scatter.6.cloned.1.call-update
  258.5 94.2 %all-reduce.3.cloned.1.call-done = f32[384,6144]{1,0:T(8,128)} async-done(((f32[384,6144]{1,0:T(8,128)}), f32[384,6144]{1,0:T(8,128)}) %all-reduce.3.cloned.1.call-update) | async-done | bytes 9437200 | tf_op jit(solution)/shard_map/psum | solution.py:57
  352.7 7.3 %fusion.17 = (f32[384]{0:T(512)S(1)}, f32[384]{0:T(512)S(1)}, f32[384,6144]{1,0:T(8,128)S(1)}, f32[384,6144]{1,0:T(8,128)S(1)}) fusion(f32[384]{0:T(512)S(1)} %add_rsqrt_fusion, f32[384]{0:T(512)S(1)} %broadcast_multiply_fusion.3, bf16[384,6144]{1,0:T(8,128)(2,1)} %copy.12, f32[384,6144]{1,0:T(8,128)} %all-reduce.3.cloned.1.call-done, ...), kind=kLoop, calls=%fused_computation.30 | loop fusion | flops 16514304 | bytes 33060864 | tf_op jit(solution)/shard_map/reduce_sum | solution.py:59
  360.1 1.6 multiply_reduce_fusion.1
  361.7 0.8 copy.13
  362.5 9.0 %psum.15 = f32[192]{0:T(256)} all-reduce(f32[192]{0:T(256)S(1)} %get-tuple-element.18), channel_id=1, replica_groups=mesh['row'=4,'col'=32] {'row'}, use_global_device_ids=true, to_apply=%region_7.0 | all-reduce | flops 192 | bytes 1536 | tf_op jit(solution)/shard_map/psum | solution.py:64
  371.5 79.0 %reduce-scatter.4.cloned.1.call-done = f32[384,192]{0,1:T(8,128)} async-done(((f32[384,6144]{0,1:T(8,128)}), f32[384,192]{0,1:T(8,128)}) %reduce-scatter.4.cloned.1.call-update) | async-done | bytes 294928 | tf_op jit(solution)/shard_map/reduce_scatter | solution.py:47
  450.5 1.6 convert_element_type.25
  452.1 91.4 %reduce-scatter.8.cloned.1.call-done = f32[384,1536]{1,0:T(8,128)} async-done(((f32[384,6144]{1,0:T(8,128)}), f32[384,1536]{1,0:T(8,128)}) %reduce-scatter.8.cloned.1.call-update) | async-done | bytes 2359312 | tf_op jit(solution)/shard_map/reduce_scatter | solution.py:65
  543.6 91.8 %reduce-scatter.6.cloned.1.call-done = f32[1536,384]{1,0:T(8,128)} async-done(((f32[6144,384]{1,0:T(8,128)}), f32[1536,384]{1,0:T(8,128)}) %reduce-scatter.6.cloned.1.call-update) | async-done | bytes 2359312 | tf_op jit(solution)/shard_map/reduce_scatter | solution.py:68
  (5 shorter events, 0.0 us)
Async XLA Ops:
  7.2 131.4 %all-gather.5.cloned.1.call-start = ((), (), s32[]{:S(2)}) async-start(), calls=%async_computation.3 | async-start | bytes 4866048 | tf_op jit(solution)/shard_map/all_gather | solution.py:30
  7.9 144.2 %all-gather.7.cloned.1.call-start = ((), (), s32[]{:S(2)}) async-start(), calls=%async_computation.4 | async-start | bytes 5898240 | tf_op jit(solution)/shard_map/all_gather | solution.py:41
  8.6 160.1 %all-gather.9.cloned.1.call-start = ((), (), s32[]{:S(2)}) async-start(), calls=%async_computation.5 | async-start | bytes 5898240 | tf_op jit(solution)/shard_map/all_gather | solution.py:45
  9.4 209.4 %all-gather.11.cloned.1.call-start = ((), (), s32[]{:S(2)}) async-start(), calls=%async_computation.7 | async-start | bytes 4866048 | tf_op jit(solution)/shard_map/all_gather | solution.py:50
  10.0 342.8 %all-reduce.3.cloned.1.call-start = ((), (), s32[]{:S(2)}) async-start(), calls=%async_computation.8 | async-start | bytes 18874368 | tf_op jit(solution)/shard_map/psum | solution.py:57
  218.7 6.6 %copy-start = (bf16[6144,384]{1,0:T(8,128)(2,1)S(1)}, bf16[6144,384]{1,0:T(8,128)(2,1)}, u32[]{:S(2)}) copy-start(bf16[6144,384]{1,0:T(8,128)(2,1)} %all-gather.7.cloned.1.call-done) | copy-start | bytes 14155780
  230.6 219.9 %reduce-scatter.4.cloned.1.call-start = ((), (), s32[]{:S(2)}) async-start(), calls=%async_computation.6 | async-start | bytes 9732096 | tf_op jit(solution)/shard_map/reduce_scatter | solution.py:47
  240.1 303.5 %reduce-scatter.8.cloned.1.call-start = ((), (), s32[]{:S(2)}) async-start(), calls=%async_computation.10 | async-start | bytes 11796480 | tf_op jit(solution)/shard_map/reduce_scatter | solution.py:65
  249.0 386.4 %reduce-scatter.6.cloned.1.call-start = ((), (), s32[]{:S(2)}) async-start(), calls=%async_computation.9 | async-start | bytes 11796480 | tf_op jit(solution)/shard_map/reduce_scatter | solution.py:68
Sparse Core Ops, SparseCore 0:
  10.3 50.6 all-gather.4
  62.6 51.4 all-gather.6
  115.8 52.9 all-gather.8
  170.9 47.8 all-gather.10
  230.7 121.9 all-reduce.2
  356.8 93.6 reduce-scatter.3
  453.5 89.9 reduce-scatter.7
  546.6 88.7 reduce-scatter.5
where the time goes:
time: 643 us; the launch traced here: 642 us
  waiting for transfers between devices  420 us (65%)
  blocking collectives  135 us (21%)
  matrix products  45.5 us (7%)
  other arithmetic  17.4 us (3%)
  between operations  14.9 us (2%)
  local copies, waits for them, and re-layouts  9.6 us (1%)
    unnamed x1, blocking collectives  126 us
    psum x1, waiting for transfers between devices, body(): grad_full = lax.psum(grad_partial, 'col')  94.2 us
    reduce_scatter x1, waiting for transfers between devices, body(): lax.psum_scatter(contract_rows(normed, grad_pre), 'row', scatter_dimensio...  91.8 us
    reduce_scatter x1, waiting for transfers between devices, body(): lax.psum_scatter(contract_rows(activated, cot_full), 'row', scatter_dimen...  91.4 us
    reduce_scatter x1, waiting for transfers between devices, body(): lax.psum_scatter(partial_value, 'col', scatter_dimension=1, tiled=True)  79 us
    all_gather x1, waiting for transfers between devices, body(): cot_full = lax.all_gather(cotangent, 'col', axis=1, tiled=True)  50 us
    dot_general x2, matrix products, contract_rows(): lax.dot_general(left, right, (((0,), (0,)), ((), ())), preferred_element_...  18.1 us
  transfers between devices with their start and end apart: 8, of which 6 were waited for; matrix products, arithmetic and copies ran while one was open for 9% of the time, Pallas kernels for 0%

commit v1 on v0

v1 whole, which is shorter than its diff:
```python
import jax
import jax.numpy as jnp
from jax import lax
from jax.sharding import PartitionSpec as P

inv_sqrt_two = 0.7071067811865476
inv_sqrt_tau = 0.3989422804014327
ROWS = 4
SHARES = 8


def gelu_parts(hidden_pre):
    cumulative = 0.5 * (1.0 + lax.erf(hidden_pre * inv_sqrt_two))
    density = jnp.exp(-0.5 * hidden_pre * hidden_pre) * inv_sqrt_tau
    return (hidden_pre * cumulative, cumulative + hidden_pre * density)


def contract_rows(left, right):
    return lax.dot_general(
        left, right, (((0,), (0,)), ((), ())), preferred_element_type=jnp.float32
    )


def contract_cols(left, right):
    return lax.dot_general(
        left, right, (((1,), (1,)), ((), ())), preferred_element_type=jnp.float32
    )


def swap_pairs():
    pairs = []
    for y in range(ROWS):
        for z in range(ROWS):
            for s in range(SHARES):
                pairs.append((y * 32 + z * 8 + s, z * 32 + y * 8 + s))
    return pairs


def swap(share):
    return lax.ppermute(share, ("row", "col"), swap_pairs())


def chunk_of(share):
    rows, width = share.shape
    pieces = lax.all_gather(swap(share), "col", axis=0)
    pieces = pieces.reshape(ROWS, SHARES, rows, width)
    return pieces.transpose(0, 2, 1, 3).reshape(ROWS * rows, SHARES * width)


def share_of(partial):
    rows, width = partial.shape[0] // ROWS, partial.shape[1] // SHARES
    pieces = partial.reshape(ROWS, rows, SHARES, width).transpose(0, 2, 1, 3)
    pieces = pieces.reshape(ROWS * SHARES, rows, width).astype(jnp.bfloat16)
    summed = lax.psum_scatter(pieces, "col", scatter_dimension=0)
    return swap(summed).astype(jnp.float32)


def body(tokens, norm_gain, inner_weight, outer_weight, cotangent):
    width = tokens.shape[1]
    features = width * 32
    cot_chunk = chunk_of(cotangent)
    values = tokens.astype(jnp.float32)
    own_mean = jnp.mean(values, axis=1, keepdims=True)
    own_second = jnp.sum((values - own_mean) ** 2, axis=1, keepdims=True)
    stats = lax.all_gather(jnp.concatenate([own_mean, own_second], axis=1), "col", axis=0)
    row_mean = jnp.mean(stats[:, :, 0], axis=0)[:, None]
    spread = (stats[:, :, 0] - row_mean[:, 0]) ** 2
    variance = (jnp.sum(stats[:, :, 1], axis=0) + width * jnp.sum(spread, axis=0))[:, None] / features
    inv_std = lax.rsqrt(variance + 1e-06)
    unit_rows = (values - row_mean) * inv_std
    gain_values = norm_gain.astype(jnp.float32)
    normed = chunk_of((unit_rows * gain_values).astype(jnp.bfloat16))
    hidden_part = jnp.dot(normed, inner_weight, preferred_element_type=jnp.float32)
    hidden_pre = lax.psum_scatter(
        hidden_part, "row", scatter_dimension=0, tiled=True
    )
    gelu_value, gelu_slope = gelu_parts(hidden_pre)
    activated = lax.all_gather(gelu_value.astype(jnp.bfloat16), "row", axis=0, tiled=True)
    act_part = contract_cols(cot_chunk, outer_weight)
    grad_act = lax.psum_scatter(
        act_part, "row", scatter_dimension=0, tiled=True
    )
    grad_pre = lax.all_gather(
        (grad_act * gelu_slope).astype(jnp.bfloat16), "row", axis=0, tiled=True
    )
    branch_out = share_of(
        jnp.dot(activated, outer_weight, preferred_element_type=jnp.float32)
    ).astype(jnp.bfloat16)
    grad_normed = share_of(contract_cols(grad_pre, inner_weight))
    grad_outer = contract_rows(activated, cot_chunk)
    grad_inner = contract_rows(normed, grad_pre)
    grad_gain = lax.psum(jnp.sum(grad_normed * unit_rows, axis=0), "row")
    grad_hat = grad_normed * gain_values
    sums = lax.psum(
        jnp.stack([jnp.sum(grad_hat, axis=1), jnp.sum(grad_hat * unit_rows, axis=1)]), "col"
    )
    first_mean = sums[0][:, None] / features
    second_mean = sums[1][:, None] / features
    grad_tokens = (inv_std * (grad_hat - first_mean - unit_rows * second_mean)).astype(
        jnp.bfloat16
    )
    return (branch_out, grad_tokens, grad_gain, grad_inner, grad_outer)


def solution(mesh):
    return jax.shard_map(
        body,
        mesh=mesh,
        in_specs=(P("row", "col"), P("col"), P("row", "col"), P("col", "row"), P("row", "col")),
        out_specs=(P("row", "col"), P("row", "col"), P("col"), P("row", "col"), P("col", "row")),
        check_vma=False,
    )
```

time: 643 us -> 517 us (0.80)
  waiting for transfers between devices: 420 us -> 276 us
  local copies, waits for them, and re-layouts: 9.6 us -> 62.2 us
  blocking collectives: 135 us -> 118 us
  matrix products: 45.5 us -> 32 us
  other arithmetic: 17.4 us -> 6.99 us
    unnamed x1 -> x0, blocking collectives: 126 us -> none
    psum x1 -> x0, waiting for transfers between devices: 94.2 us -> none  [body(): grad_full = lax.psum(grad_partial, 'col')]
    reduce_scatter x3 -> x4, waiting for transfers between devices: 262 us -> 188 us  [the longest x2 132 us: share_of(): summed = lax.psum_scatter(pieces, 'col', scatter_dimension=0)]
    psum x1 -> x2, blocking collectives: 8.98 us -> 78 us  [the longest x1 66.6 us: body(): lax.psum(jnp.stack([jnp.sum(grad_hat, axis=1), jnp.sum(grad_hat * unit_ro...]
    convert_element_type x0 -> x6, local copies, waits for them, and re-layouts: none -> 42.6 us  [share_of(): pieces = pieces.reshape(ROWS * SHARES, rows, width).astype(jnp.bfloat16)]
    all_gather x0 -> x1, blocking collectives: none -> 39.7 us  [body(): lax.all_gather(jnp.concatenate([own_mean, own_second], axis=1), 'col', ax...]
    all_gather x4, waiting for transfers between devices: 60.5 us -> 87.9 us  [the longest x2 65.2 us: chunk_of(): pieces = lax.all_gather(swap(share), 'col', axis=0)]
    reduce_sum x4 -> x5, other arithmetic: 15.7 us -> 2.14 us  [the longest x1 0.97 us: body(): own_second = jnp.sum((values - own_mean) ** 2, axis=1, keepdims=True)]
  transfers between devices with their start and end apart: 8 -> 12, of which waited for: 6 -> 7; matrix products, arithmetic and copies ran while one was open for 9% -> 18% of each run, Pallas kernels for 0% -> 0%
where the time goes in v1:
time: 517 us; the launch traced here: 516 us
  waiting for transfers between devices  276 us (53%)
  blocking collectives  118 us (23%)
  local copies, waits for them, and re-layouts  62.2 us (12%)
  matrix products  32 us (6%)
  between operations  14.3 us (3%)
  other arithmetic  6.99 us (1%)
  starting transfers between devices  6.34 us (1%)
    reduce_scatter x2, waiting for transfers between devices, share_of(): summed = lax.psum_scatter(pieces, 'col', scatter_dimension=0)  132 us
    psum x1, blocking collectives, body(): lax.psum(jnp.stack([jnp.sum(grad_hat, axis=1), jnp.sum(grad_hat * unit_ro...  66.6 us
    all_gather x2, waiting for transfers between devices, chunk_of(): pieces = lax.all_gather(swap(share), 'col', axis=0)  65.2 us
    convert_element_type x6, local copies, waits for them, and re-layouts, share_of(): pieces = pieces.reshape(ROWS * SHARES, rows, width).astype(jnp.bfloat16)  42.6 us
    all_gather x1, blocking collectives, body(): lax.all_gather(jnp.concatenate([own_mean, own_second], axis=1), 'col', ax...  39.7 us
    reduce_scatter x1, waiting for transfers between devices, body(): lax.psum_scatter(hidden_part, 'row', scatter_dimension=0, tiled=True)  34.4 us
    all_gather x1, waiting for transfers between devices, body(): lax.all_gather((grad_act * gelu_slope).astype(jnp.bfloat16), 'row', axis=...  22.6 us
    reduce_scatter x1, waiting for transfers between devices, body(): lax.psum_scatter(act_part, 'row', scatter_dimension=0, tiled=True)  21.6 us
  transfers between devices with their start and end apart: 12, of which 7 were waited for; matrix products, arithmetic and copies ran while one was open for 18% of the time, Pallas kernels for 0%

profile of v1, /device:TPU:1, one launch (start us, length us, event | category | flops | bytes accessed | tf_op | source)
XLA Modules:
  0.0 516.1 jit_solution(1703489023285843581)
XLA Ops:
  7.2 0.0 copy-start
  7.2 0.0 all-gather.14.cloned.1.call-start
  7.2 1.7 collective-permute-start.2
  8.9 0.7 copy-done.5
  9.6 0.0 all-gather.14.cloned.1.call-update
  9.6 0.0 all-gather.12.cloned.1.call-start
  9.7 0.7 convert_element_type.48
  10.3 1.0 convert_reduce_fusion
  11.3 1.0 fusion.15
  12.3 39.7 %all-gather = f32[12288,2]{0,1:T(2,128)S(1)} all-gather(f32[384,2]{0,1:T(2,128)S(1)} %pad_maximum_fusion), channel_id=2, replica_groups=mesh['row'=4,'col'=32] {'col'}, dimensions={0}, use_global_device_ids=true | all-gather | bytes 101376 | tf_op jit(solution)/shard_map/all_gather | solution.py:65
  52.1 1.0 fusion.19
  53.1 0.7 collective-permute-start
  53.8 0.0 copy-start.6
  53.8 0.7 copy-done.6
  54.5 0.0 all-gather.12.cloned.1.call-update
  54.5 0.0 reduce-scatter.9.cloned.1.call-start
  54.5 23.8 %all-gather.14.cloned.1.call-done = bf16[12288,192]{0,1:T(8,128)(2,1)} async-done(((bf16[384,192]{0,1:T(8,128)(2,1)}), bf16[12288,192]{0,1:T(8,128)(2,1)}) %all-gather.14.cloned.1.call-update) | async-done | bytes 4718608 | tf_op jit(solution)/shard_map/all_gather | solution.py:45
  78.3 3.3 copy.25
  81.6 1.8 copy.19
  83.5 0.9 copy.26
  84.3 2.1 copy-done.2
  86.5 4.1 fusion.25
  90.6 0.0 reduce-scatter.9.cloned.1.call-update
  90.6 0.2 reduce-scatter.5.cloned.1.call-start
  90.8 41.5 %all-gather.12.cloned.1.call-done = bf16[12288,192]{0,1:T(8,128)(2,1)} async-done(((bf16[384,192]{0,1:T(8,128)(2,1)}), bf16[12288,192]{0,1:T(8,128)(2,1)}) %all-gather.12.cloned.1.call-update) | async-done | bytes 4718608 | tf_op jit(solution)/shard_map/all_gather | solution.py:45
  132.3 3.3 copy.23
  135.6 1.8 copy.16
  137.5 0.9 copy.24
  138.3 2.2 copy-done.3
  140.5 4.1 fusion.24
  144.6 0.0 reduce-scatter.5.cloned.1.call-update
  144.6 0.0 all-gather.10.cloned.1.call-start
  144.7 21.6 %reduce-scatter.9.cloned.1.call-done = f32[384,384]{1,0:T(8,128)} async-done(((f32[1536,384]{1,0:T(8,128)}), f32[384,384]{1,0:T(8,128)}) %reduce-scatter.9.cloned.1.call-update) | async-done | bytes 589840 | tf_op jit(solution)/shard_map/reduce_scatter | solution.py:80
  166.3 34.4 %reduce-scatter.5.cloned.1.call-done = f32[384,384]{1,0:T(8,128)} async-done(((f32[1536,384]{1,0:T(8,128)}), f32[384,384]{1,0:T(8,128)}) %reduce-scatter.5.cloned.1.call-update) | async-done | bytes 589840 | tf_op jit(solution)/shard_map/reduce_scatter | solution.py:74
  200.7 2.3 fusion.5
  203.0 0.0 all-gather.10.cloned.1.call-update
  203.0 0.0 all-gather.8.cloned.1.call-start
  203.1 0.5 all-gather.8.cloned.1.call-update
  203.6 0.0 reduce-scatter.11.cloned.1.call-start
  203.7 22.6 %all-gather.10.cloned.1.call-done = bf16[1536,384]{1,0:T(8,128)(2,1)} async-done(((bf16[384,384]{1,0:T(8,128)(2,1)}), bf16[1536,384]{1,0:T(8,128)(2,1)}) %all-gather.10.cloned.1.call-update) | async-done | bytes 1179664 | tf_op jit(solution)/shard_map/all_gather | solution.py:83
  226.3 5.6 %convolution_convert_fusion = bf16[1536,1536]{1,0:T(8,128)(2,1)} fusion(bf16[1536,384]{1,0:T(8,128)(2,1)} %all-gather.10.cloned.1.call-done, bf16[1536,384]{1,0:T(8,128)(2,1)S(1)} %copy-done), kind=kOutput, calls=%fused_computation | convolution fusion | flops 1814298624 | bytes 7077888 | tf_op jit(solution)/shard_map/dot_general | solution.py:25
  231.9 6.6 %copy.20 = bf16[1536,1536]{0,1:T(8,128)(2,1)} copy(bf16[1536,1536]{1,0:T(8,128)(2,1)} %convolution_convert_fusion) | data formatting | bytes 9437184 | tf_op jit(solution)/shard_map/convert_element_type | solution.py:53
  238.6 9.1 %convert_element_type.57 = bf16[4,384,8,192]{1,0,3,2:T(4,128)(2,1)} reshape(bf16[1536,1536]{0,1:T(8,128)(2,1)} %copy.20) | data formatting | bytes 9437184 | tf_op jit(solution)/shard_map/convert_element_type | solution.py:53
  247.6 5.5 %copy.21 = bf16[4,8,384,192]{2,3,1,0:T(8,128)(2,1)} copy(bf16[4,8,384,192]{2,0,3,1:T(4,128)(2,1)} %bitcast.62) | data formatting | bytes 9437184 | tf_op jit(solution)/shard_map/convert_element_type | solution.py:53
  253.2 0.0 reduce-scatter.11.cloned.1.call-update
  253.2 0.3 reduce-scatter.7.cloned.1.call-start
  253.5 0.0 all-gather.8.cloned.1.call-done
  253.5 5.6 %convolution_convert_fusion.1 = bf16[1536,1536]{1,0:T(8,128)(2,1)} fusion(bf16[1536,384]{1,0:T(8,128)(2,1)} %all-gather.8.cloned.1.call-done, bf16[384,1536]{1,0:T(8,128)(2,1)S(1)} %copy-done.7), kind=kOutput, calls=%fused_computation.1 | convolution fusion | flops 1814298624 | bytes 7077888 | tf_op jit(solution)/shard_map/dot_general | solution.py:87
  259.1 6.7 %copy.17 = bf16[1536,1536]{0,1:T(8,128)(2,1)} copy(bf16[1536,1536]{1,0:T(8,128)(2,1)} %convolution_convert_fusion.1) | data formatting | bytes 9437184 | tf_op jit(solution)/shard_map/convert_element_type | solution.py:53
  265.8 9.1 %convert_element_type.52 = bf16[4,384,8,192]{1,0,3,2:T(4,128)(2,1)} reshape(bf16[1536,1536]{0,1:T(8,128)(2,1)} %copy.17) | data formatting | bytes 9437184 | tf_op jit(solution)/shard_map/convert_element_type | solution.py:53
  274.9 5.5 %copy.18 = bf16[4,8,384,192]{2,3,1,0:T(8,128)(2,1)} copy(bf16[4,8,384,192]{2,0,3,1:T(4,128)(2,1)} %bitcast.63) | data formatting | bytes 9437184 | tf_op jit(solution)/shard_map/convert_element_type | solution.py:53
  280.4 0.0 reduce-scatter.7.cloned.1.call-update
  280.5 1.3 copy-done.8
  281.8 6.6 %fusion.26 = f32[1536,384]{1,0:T(8,128)} fusion(bf16[1536,1536]{0,1:T(8,128)(2,1)} %bitcast.67, bf16[1536,384]{1,0:T(8,128)(2,1)S(1)} %copy-done.8), kind=kOutput, calls=%fused_computation.47 | convolution fusion | flops 1811939328 | bytes 8257536 | tf_op jit(solution)/shard_map/dot_general | solution.py:19
  288.4 52.4 %reduce-scatter.11.cloned.1.call-done = bf16[1,384,192]{1,2,0:T(8,128)(2,1)} async-done(((bf16[32,384,192]{1,2,0:T(8,128)(2,1)}), bf16[1,384,192]{1,2,0:T(8,128)(2,1)}) %reduce-scatter.11.cloned.1.call-update) | async-done | bytes 147472 | tf_op jit(solution)/shard_map/reduce_scatter | solution.py:54
  340.8 1.7 collective-permute-start.3
  342.5 5.9 %fusion.27 = f32[384,1536]{1,0:T(8,128)} fusion(bf16[1536,384]{1,0:T(8,128)(2,1)S(1)} %copy-done.9, bf16[1536,1536]{0,1:T(8,128)(2,1)} %bitcast.65), kind=kOutput, calls=%fused_computation.48 | convolution fusion | flops 1811939328 | bytes 8257536 | tf_op jit(solution)/shard_map/dot_general | solution.py:19
  348.4 79.5 %reduce-scatter.7.cloned.1.call-done = bf16[1,384,192]{1,2,0:T(8,128)(2,1)} async-done(((bf16[32,384,192]{1,2,0:T(8,128)(2,1)}), bf16[1,384,192]{1,2,0:T(8,128)(2,1)}) %reduce-scatter.7.cloned.1.call-update) | async-done | bytes 147472 | tf_op jit(solution)/shard_map/reduce_scatter | solution.py:54
  428.0 1.6 collective-permute-start.1
  429.5 0.2 fusion.13
  429.7 11.4 %psum.15 = f32[192]{0:T(256)} all-reduce(f32[192]{0:T(256)S(1)} %get-tuple-element.5), channel_id=1, replica_groups=mesh['row'=4,'col'=32] {'row'}, use_global_device_ids=true, to_apply=%region_13.0 | all-reduce | flops 192 | bytes 1536 | tf_op jit(solution)/shard_map/psum | solution.py:92
  441.2 66.6 %psum.14 = f32[2,384]{1,0:T(2,128)S(1)} all-reduce(f32[2,384]{1,0:T(2,128)S(1)} %pad_maximum_fusion.1), channel_id=1, replica_groups=mesh['row'=4,'col'=32] {'col'}, use_global_device_ids=true, to_apply=%region_11.0 | all-reduce | flops 768 | bytes 6144 | tf_op jit(solution)/shard_map/psum | solution.py:94
  507.8 0.8 fusion.12
  508.6 0.7 copy.30
  (30 shorter events, 0.2 us)
Async XLA Ops:
  7.2 133.3 %copy-start = (bf16[1536,384]{1,0:T(8,128)(2,1)S(1)}, bf16[1536,384]{1,0:T(8,128)(2,1)}, u32[]{:S(2)}) copy-start(bf16[1536,384]{1,0:T(8,128)(2,1)} %param.7) | copy-start | bytes 3538948
  7.2 71.1 %all-gather.14.cloned.1.call-start = ((), (), s32[]{:S(2)}) async-start(), calls=%async_computation.11 | async-start | bytes 4866048 | tf_op jit(solution)/shard_map/all_gather | solution.py:45
  7.2 1.7 collective-permute-start.2
  8.9 0.7 copy-start.5
  9.6 122.7 %all-gather.12.cloned.1.call-start = ((), (), s32[]{:S(2)}) async-start(), calls=%async_computation.10 | async-start | bytes 4866048 | tf_op jit(solution)/shard_map/all_gather | solution.py:45
  53.1 0.7 collective-permute-start
  53.8 0.7 copy-start.6
  54.5 111.8 %reduce-scatter.9.cloned.1.call-start = ((), (), s32[]{:S(2)}) async-start(), calls=%async_computation.7 | async-start | bytes 2949120 | tf_op jit(solution)/shard_map/reduce_scatter | solution.py:80
  83.5 3.0 copy-start.7
  84.3 2.1 copy-start.2
  90.6 110.1 %reduce-scatter.5.cloned.1.call-start = ((), (), s32[]{:S(2)}) async-start(), calls=%async_computation.4 | async-start | bytes 2949120 | tf_op jit(solution)/shard_map/reduce_scatter | solution.py:74
  138.3 2.2 copy-start.3
  144.6 81.7 %all-gather.10.cloned.1.call-start = ((), (), s32[]{:S(2)}) async-start(), calls=%async_computation.8 | async-start | bytes 1474560 | tf_op jit(solution)/shard_map/all_gather | solution.py:83
  203.0 50.5 %all-gather.8.cloned.1.call-start = ((), (), s32[]{:S(2)}) async-start(), calls=%async_computation.5 | async-start | bytes 1474560 | tf_op jit(solution)/shard_map/all_gather | solution.py:78
  203.6 137.2 %reduce-scatter.11.cloned.1.call-start = ((), (), s32[]{:S(2)}) async-start(), calls=%async_computation.9 | async-start | bytes 4866048 | tf_op jit(solution)/shard_map/reduce_scatter | solution.py:54
  253.2 174.7 %reduce-scatter.7.cloned.1.call-start = ((), (), s32[]{:S(2)}) async-start(), calls=%async_computation.6 | async-start | bytes 4866048 | tf_op jit(solution)/shard_map/reduce_scatter | solution.py:54
  280.4 1.3 copy-start.8
  281.8 60.7 %copy-start.9 = (bf16[1536,384]{1,0:T(8,128)(2,1)S(1)}, bf16[1536,384]{1,0:T(8,128)(2,1)}, u32[]{:S(2)}) copy-start(bf16[1536,384]{1,0:T(8,128)(2,1)} %all-gather.8.cloned.1.call-done) | copy-start | bytes 3538948
  340.8 88.7 %copy-start.4 = (bf16[384,192]{0,1:T(8,128)(2,1)S(1)}, bf16[384,192]{0,1:T(8,128)(2,1)}, u32[]{:S(2)}) copy-start(bf16[384,192]{0,1:T(8,128)(2,1)} %param.5) | copy-start | bytes 442372
  340.8 88.7 %collective-permute-start.3 = (bf16[384,192]{0,1:T(8,128)(2,1)}, bf16[384,192]{0,1:T(8,128)(2,1)S(1)}, u32[]{:S(2)}, u32[]{:S(2)}) collective-permute-start(bf16[384,192]{0,1:T(8,128)(2,1)} %bitcast.74), channel_id=1, source_target_pairs={{0,0},{1,1},{2,2},{3,3},{4,4},{5,5},{6,6},{7,7},{8,32},{9,33},{10,... | collective-permute-start | bytes 442376 | tf_op jit(solution)/shard_map/ppermute | solution.py:40
  342.5 166.7 %copy-start.1 = (bf16[1536,384]{1,0:T(8,128)(2,1)S(1)}, bf16[1536,384]{1,0:T(8,128)(2,1)}, u32[]{:S(2)}) copy-start(bf16[1536,384]{1,0:T(8,128)(2,1)} %param.7) | copy-start | bytes 3538948
  428.0 79.8 %collective-permute-start.1 = (bf16[384,192]{0,1:T(8,128)(2,1)}, bf16[384,192]{0,1:T(8,128)(2,1)S(1)}, u32[]{:S(2)}, u32[]{:S(2)}) collective-permute-start(bf16[384,192]{0,1:T(8,128)(2,1)} %bitcast.73), channel_id=1, source_target_pairs={{0,0},{1,1},{2,2},{3,3},{4,4},{5,5},{6,6},{7,7},{8,32},{9,33},{10,... | collective-permute-start | bytes 442376 | tf_op jit(solution)/shard_map/ppermute | solution.py:40
Sparse Core Ops, SparseCore 0:
  10.8 67.4 all-gather.13
  81.0 51.2 all-gather.11
  135.3 30.9 reduce-scatter.8
  169.1 31.5 reduce-scatter.4
  203.2 23.0 all-gather.9
  228.4 24.9 all-gather.7
  257.1 83.6 reduce-scatter.10
  345.0 82.9 reduce-scatter.6

commit v2 on v0

v2 whole, which is shorter than its diff:
```python
import jax
import jax.numpy as jnp
from jax import lax
from jax.experimental import pallas as pl
from jax.experimental.pallas import tpu as pltpu
from jax.sharding import PartitionSpec as P

inv_sqrt_two = 0.7071067811865476
inv_sqrt_tau = 0.3989422804014327
MESH = pl.DeviceIdType.MESH
BF16 = jnp.bfloat16
F32 = jnp.float32

ROWS, SHARE = 384, 192
HALF, QUARTER = 192, 96
GROUP, CHUNK = 384, 1536
HID, PAIR = 384, 768
FEATURES = 6144
COPIES = 160


def gelu_parts(hidden_pre):
    cumulative = 0.5 * (1.0 + lax.erf(hidden_pre * inv_sqrt_two))
    density = jnp.exp(-0.5 * hidden_pre * hidden_pre) * inv_sqrt_tau
    return (hidden_pre * cumulative, cumulative + hidden_pre * density)


def dot_nn(left, right):
    return jnp.dot(left, right, preferred_element_type=F32)


def dot_nt(left, right):
    return lax.dot_general(
        left, right, (((1,), (1,)), ((), ())), preferred_element_type=F32
    )


def dot_tn(left, right):
    return lax.dot_general(
        left, right, (((0,), (0,)), ((), ())), preferred_element_type=F32
    )


def turn(index, by):
    return lax.rem(index + (by % 4), 4)


def to_rows(first, second):
    lane = lax.broadcasted_iota(jnp.int32, (ROWS, 128), 1)
    both = jnp.where(lane == 0, first, jnp.where(lane == 1, second, 0.0))
    return both.T[:8]


def to_columns(rows):
    full = jnp.concatenate([rows, jnp.zeros((120, ROWS), F32)], axis=0).T
    return full[:, 0:1], full[:, 1:2]


def merge_moments(parts, count):
    mean = sum(p[0:1] for p in parts) * (1.0 / len(parts))
    second = sum(p[1:2] + count * (p[0:1] - mean) ** 2 for p in parts)
    return jnp.concatenate([mean, second, jnp.zeros((6, ROWS), F32)], axis=0)


def kernel(
    tok_ref, gain_ref, w_in, w_out, cot_ref,
    branch_ref, gtok_ref, ggain_ref, ginner_ref, gouter_ref,
    w1, w2, unit, stat, tail, ggbuf,
    give_tok, mrg_tok, mrg_cot, own_tok, own_cot, g_tok, g_cot, n_tok, n_cot,
    hf, hb_tok, hb_cot, y1_tok, y1_cot, y2_tok, y2_cot, h_tok, h_cot,
    act, gpre,
    pb_out, pb_gn, r1_out, r1_gn, r2_out, r2_gn, s_out, s_gn, r3_out, r3_gn, r4_out, r4_gn,
    f_out, f_gn, o_out, o_gn, c_out, c_gn, d_out, d_gn,
    go_own, go_send, go_recv, gi_own, gi_send, gi_recv,
    send_sem, recv_sem, local_sem,
):
    y = lax.axis_index("row")
    col = lax.axis_index("col")
    z, x, q = col // 8, lax.rem(col // 2, 4), lax.rem(col, 2)
    p = 1 - q
    a0, b0 = p * x + q * z, p * z + q * x
    am, ap, a2 = turn(a0, -1), turn(a0, 1), turn(a0, 2)
    bm, bp, b2 = turn(b0, -1), turn(b0, 1), turn(b0, 2)
    ym, yp, y2 = turn(y, -1), turn(y, 1), turn(y, 2)
    first, second = q == 0, y != z

    def device(yy, zz, xx, qq):
        return (yy, zz * 8 + xx * 2 + qq)

    def on_a(by):
        return device(y, lax.rem(z + q * (by % 4), 4), lax.rem(x + p * (by % 4), 4), q)

    def on_b(by):
        return device(y, lax.rem(z + p * (by % 4), 4), lax.rem(x + q * (by % 4), 4), q)

    def on_y(by):
        return device(turn(y, by), z, x, q)

    mate = device(y, z, x, p)
    mirror = device(z, y, x, q)
    started, count = [], [0]

    def copy(src, dst, to):
        at = count[0]
        count[0] += 1
        return pltpu.make_async_remote_copy(
            src_ref=src, dst_ref=dst, send_sem=send_sem.at[at], recv_sem=recv_sem.at[at],
            device_id=to, device_id_type=MESH,
        )

    def send(src, dst, to):
        c = copy(src, dst, to)
        c.start()
        started.append(c)
        return c

    def rows_of(half):
        return pl.ds(pl.multiple_of(half * HALF, HALF), HALF)

    top, bottom = pl.ds(0, QUARTER), pl.ds(QUARTER, QUARTER)

    barrier = pltpu.get_barrier_semaphore()
    others = [mate] + [on(by) for on in (on_a, on_b, on_y) for by in (1, 2, 3)]
    for other in others:
        pl.semaphore_signal(barrier, inc=1, device_id=other, device_id_type=MESH)

    @pl.when(second)
    def _():
        pl.semaphore_signal(barrier, inc=1, device_id=mirror, device_id_type=MESH)
        pl.semaphore_wait(barrier, len(others) + 1)

    @pl.when(jnp.logical_not(second))
    def _():
        pl.semaphore_wait(barrier, len(others))

    give, keep = rows_of(p), rows_of(q)
    c_mrg_cot = send(cot_ref.at[give], mrg_cot, mate)
    hid_own = pl.ds(pl.multiple_of(q * HID, HID), HID)
    local_in = pltpu.make_async_copy(w_in, w1.at[:, hid_own], local_sem.at[0])
    local_out = pltpu.make_async_copy(w_out, w2.at[hid_own], local_sem.at[1])
    local_out.start()
    local_in.start()
    c_w2 = send(w_out, w2.at[hid_own], mate)
    c_w1 = send(w_in, w1.at[:, hid_own], mate)

    values = tok_ref[...].astype(F32)
    own_mean = jnp.sum(values, axis=1, keepdims=True) * (1.0 / SHARE)
    own_second = jnp.sum((values - own_mean) ** 2, axis=1, keepdims=True)
    stat[0] = to_rows(own_mean, own_second)
    c_stat = [send(stat.at[0], stat.at[1], mate)]

    def joined(a_half, b_half):
        return jnp.where(
            first,
            jnp.concatenate([a_half, b_half], axis=1),
            jnp.concatenate([b_half, a_half], axis=1),
        )

    def mirrored(piece, landing, at_home):
        c = copy(piece, landing, mirror)

        @pl.when(second)
        def _():
            c.start()

        @pl.when(jnp.logical_not(second))
        def _():
            at_home[...] = piece[...]

        return c

    def mirrored_wait(c):
        @pl.when(second)
        def _():
            c.wait_recv()

    def mirrored_sent(c):
        @pl.when(second)
        def _():
            c.wait_send()

    b_there, a_there = p * y + q * x, p * x + q * y

    c_mrg_cot.wait_recv()
    own_cot[...] = joined(
        cot_ref[keep].astype(F32), mrg_cot[...].astype(F32)
    ).astype(BF16)
    m_cot = mirrored(own_cot, g_cot.at[b_there, a_there], g_cot.at[b0, a0])

    c_stat[0].wait_recv()
    stat[2] = merge_moments([stat[0], stat[1]], SHARE)
    c_stat = [send(stat.at[2], stat.at[2 + by], on_a(by)) for by in (1, 2, 3)]
    for c in c_stat:
        c.wait_recv()
    stat[6] = merge_moments([stat[2 + by] for by in range(4)], 2 * SHARE)
    c_stat = [send(stat.at[6], stat.at[6 + by], on_b(by)) for by in (1, 2, 3)]
    for c in c_stat:
        c.wait_recv()
    stat[10] = merge_moments([stat[6 + by] for by in range(4)], 8 * SHARE)
    row_mean, total_second = to_columns(stat[10])
    inv_std = lax.rsqrt(total_second * (1.0 / FEATURES) + 1e-06)
    unit[...] = (tok_ref[...].astype(F32) - row_mean) * inv_std
    gain_values = gain_ref[...].astype(F32)
    normed_give = (unit[give] * gain_values).astype(BF16)
    give_tok[...] = normed_give
    c_mrg_tok = send(give_tok, mrg_tok, mate)

    class Gather:
        def __init__(self, g):
            self.g = g

        def own(self):
            g, home = self.g, self.g.at[b0, a0]
            self.ap, self.am = send(home, home, on_a(1)), send(home, home, on_a(-1))
            self.b = [(send(home, home, on_b(1)), send(home, home, on_b(-1)))]

        def near(self):
            g = self.g
            self.ap.wait_recv()
            left = g.at[b0, am]
            self.fa_top = send(left.at[top], left.at[top], on_a(1))
            self.b.append((send(left, left, on_b(1)), send(left, left, on_b(-1))))
            self.am.wait_recv()
            right = g.at[b0, ap]
            self.fa_bottom = send(right.at[bottom], right.at[bottom], on_a(-1))
            self.b.append((send(right, right, on_b(1)), send(right, right, on_b(-1))))
            self.fb = []

        def onward(self, i):
            g, a = self.g, (a0, am, ap, a2)[i]
            self.b[i][0].wait_recv()
            left = g.at[bm, a, top]
            up = send(left, left, on_b(1))
            self.b[i][1].wait_recv()
            right = g.at[bp, a, bottom]
            down = send(right, right, on_b(-1))
            self.fb.append((up, down))

        def far(self):
            self.fa_top.wait_recv()
            self.fa_bottom.wait_recv()
            last = self.g.at[b0, a2]
            self.b.append((send(last, last, on_b(1)), send(last, last, on_b(-1))))

        def end(self):
            for up, down in self.fb:
                up.wait_recv()
                down.wait_recv()

    def lay_out(g, n):
        def step(j, _):
            for s in range(4):
                piece = g[p * j + q * s, p * s + q * j]
                n[rows_of(j), s * GROUP : (s + 1) * GROUP] = piece
            return 0

        lax.fori_loop(0, 4, step, 0)

    cot_gather, tok_gather = Gather(g_cot), Gather(g_tok)
    mirrored_wait(m_cot)
    cot_gather.own()

    c_mrg_tok.wait_recv()
    own_tok[...] = joined(unit[keep] * gain_values, mrg_tok[...].astype(F32)).astype(BF16)
    m_tok = mirrored(own_tok, g_tok.at[b_there, a_there], g_tok.at[b0, a0])

    cot_gather.near()
    cot_gather.onward(0)
    cot_gather.far()
    cot_gather.onward(1)
    mirrored_wait(m_tok)
    tok_gather.own()
    cot_gather.onward(2)
    cot_gather.onward(3)
    tok_gather.near()
    tok_gather.onward(0)
    cot_gather.end()
    tok_gather.far()

    lay_out(g_cot, n_cot)
    local_out.wait()
    c_w2.wait_recv()

    class RowSum:
        def __init__(self, hb, r1, r2):
            self.hb, self.r1, self.r2 = hb, r1, r2

        def compute(self, product):
            def step(t, _):
                j = lax.rem(y + 2 + t, 4)
                value = product(j)
                hf[j] = value
                self.hb[j] = value.astype(BF16)
                return 0

            lax.fori_loop(0, 4, step, 0)
            hb, r1, r2 = self.hb, self.r1, self.r2
            self.up1 = send(hb.at[y2, top], r1.at[0], on_y(1))
            self.down1 = send(hb.at[y2, bottom], r1.at[1], on_y(-1))
            self.up2 = send(hb.at[yp, bottom], r2.at[0, bottom], on_y(1))
            self.down2 = send(hb.at[ym, top], r2.at[1, top], on_y(-1))

        def onward(self):
            hb, r1, r2 = self.hb, self.r1, self.r2
            self.up1.wait_recv()
            hb[yp, top] = (hf[yp, top] + r1[0].astype(F32)).astype(BF16)
            self.up3 = send(hb.at[yp, top], r2.at[0, top], on_y(1))
            self.down1.wait_recv()
            hb[ym, bottom] = (hf[ym, bottom] + r1[1].astype(F32)).astype(BF16)
            self.down3 = send(hb.at[ym, bottom], r2.at[1, bottom], on_y(-1))

        def end(self, out):
            out[...] = hf[y]

        def finish(self, out):
            for c in (self.up2, self.up3, self.down2, self.down3):
                c.wait_recv()
            out[...] += self.r2[0].astype(F32) + self.r2[1].astype(F32)

    cot_sum = RowSum(hb_cot, y1_cot, y2_cot)
    tok_sum = RowSum(hb_tok, y1_tok, y2_tok)
    cot_sum.compute(lambda j: dot_nt(n_cot[rows_of(j)], w2[...]))
    tok_gather.onward(1)
    tok_gather.onward(2)
    cot_sum.onward()
    cot_sum.end(h_cot)
    tok_gather.onward(3)
    tok_gather.end()
    lay_out(g_tok, n_tok)
    local_in.wait()
    c_w1.wait_recv()
    tok_sum.compute(lambda j: dot_nn(n_tok[rows_of(j)], w1[...]))
    cot_sum.finish(h_cot)
    tok_sum.onward()
    tok_sum.end(h_tok)
    tok_sum.finish(h_tok)

    gelu_value, gelu_slope = gelu_parts(h_tok[...])
    act[y] = gelu_value.astype(BF16)
    gpre[y] = (h_cot[...] * gelu_slope).astype(BF16)

    class RowGather:
        def __init__(self, g):
            self.g = g
            self.up, self.down = send(g.at[y], g.at[y], on_y(1)), send(g.at[y], g.at[y], on_y(-1))

        def onward(self):
            g = self.g
            self.up.wait_recv()
            self.fup = send(g.at[ym, top], g.at[ym, top], on_y(1))
            self.down.wait_recv()
            self.fdown = send(g.at[yp, bottom], g.at[yp, bottom], on_y(-1))

        def end(self):
            self.fup.wait_recv()
            self.fdown.wait_recv()

    act_gather = RowGather(act)
    gpre_gather = RowGather(gpre)
    act_gather.onward()
    act_gather.end()
    gpre_gather.onward()

    class PlaneSum:
        def __init__(self, pb, r1, r2, s, r3, r4, f):
            self.pb, self.r1, self.r2, self.s = pb, r1, r2, s
            self.r3, self.r4, self.f = r3, r4, f

        def compute(self, product):
            pb, r1, r2 = self.pb, self.r1, self.r2

            def step(j, _):
                value = product(j).astype(BF16)
                for s in range(4):
                    pb[p * j + q * s, p * s + q * j] = value[:, s * GROUP : (s + 1) * GROUP]
                return 0

            lax.fori_loop(0, 4, step, 0)
            self.up1 = send(pb.at[b2, :, top], r1.at[0], on_b(1))
            self.down1 = send(pb.at[b2, :, bottom], r1.at[1], on_b(-1))
            self.up2 = send(pb.at[bp, :, bottom], r2.at[0, :, bottom], on_b(1))
            self.down2 = send(pb.at[bm, :, top], r2.at[1, :, top], on_b(-1))

        def onward(self):
            pb, r1, r2 = self.pb, self.r1, self.r2
            self.up1.wait_recv()
            pb[bp, :, top] = (pb[bp, :, top].astype(F32) + r1[0].astype(F32)).astype(BF16)
            self.up3 = send(pb.at[bp, :, top], r2.at[0, :, top], on_b(1))
            self.down1.wait_recv()
            pb[bm, :, bottom] = (pb[bm, :, bottom].astype(F32) + r1[1].astype(F32)).astype(BF16)
            self.down3 = send(pb.at[bm, :, bottom], r2.at[1, :, bottom], on_b(-1))

        def cross(self):
            pb, r2, s, r3, r4 = self.pb, self.r2, self.s, self.r3, self.r4
            for c in (self.up2, self.down2, self.up3, self.down3):
                c.wait_recv()

            def summed(a):
                return pb[b0, a].astype(F32) + r2[0, a].astype(F32) + r2[1, a].astype(F32)

            s[a2] = summed(a2).astype(BF16)
            self.up4 = send(s.at[a2, top], r3.at[0], on_a(1))
            self.down4 = send(s.at[a2, bottom], r3.at[1], on_a(-1))
            s[ap] = summed(ap).astype(BF16)
            self.up5 = send(s.at[ap, bottom], r4.at[0, bottom], on_a(1))
            s[am] = summed(am).astype(BF16)
            self.down5 = send(s.at[am, top], r4.at[1, top], on_a(-1))
            self.f[...] = summed(a0)

        def near(self):
            s, r3, r4 = self.s, self.r3, self.r4
            self.up4.wait_recv()
            s[ap, top] = (s[ap, top].astype(F32) + r3[0].astype(F32)).astype(BF16)
            self.up6 = send(s.at[ap, top], r4.at[0, top], on_a(1))
            self.down4.wait_recv()
            s[am, bottom] = (s[am, bottom].astype(F32) + r3[1].astype(F32)).astype(BF16)
            self.down6 = send(s.at[am, bottom], r4.at[1, bottom], on_a(-1))

        def end(self):
            for c in (self.up5, self.down5, self.up6, self.down6):
                c.wait_recv()
            return self.f[...] + self.r4[0].astype(F32) + self.r4[1].astype(F32)

    out_sum = PlaneSum(pb_out, r1_out, r2_out, s_out, r3_out, r4_out, f_out)
    gn_sum = PlaneSum(pb_gn, r1_gn, r2_gn, s_gn, r3_gn, r4_gn, f_gn)
    out_sum.compute(lambda j: dot_nn(act[j], w2[...]))
    gpre_gather.end()
    gn_sum.compute(lambda j: dot_nt(gpre[j], w1[...]))
    out_sum.onward()

    def by_hidden(t, who):
        return pl.ds(pl.multiple_of(who * HID, HID), HID)

    def grad_outer(who, into):
        left = act[:, :, by_hidden(0, who)].reshape(4 * HALF, HID)
        into[...] = dot_tn(left, n_cot[...])

    def grad_inner(who, into):
        right = gpre[:, :, by_hidden(0, who)].reshape(4 * HALF, HID)

        def step(t, _):
            at = pl.ds(pl.multiple_of(t * GROUP, GROUP), GROUP)
            into[at] = dot_tn(n_tok[:, at], right)
            return 0

        lax.fori_loop(0, 4, step, 0)

    grad_outer(p, go_send)
    c_go = send(go_send, go_recv, mate)
    out_sum.cross()
    gn_sum.onward()
    grad_inner(p, gi_send)
    c_gi = send(gi_send, gi_recv, mate)
    out_sum.near()
    out_total = out_sum.end()
    f_piece_out = s_out.at[a0]
    s_out[a0] = out_total.astype(BF16)
    m_out = mirrored(f_piece_out, o_out, o_out)
    gn_sum.cross()
    grad_outer(q, go_own)
    gn_sum.near()
    gn_total = gn_sum.end()
    s_gn[a0] = gn_total.astype(BF16)
    m_gn = mirrored(s_gn.at[a0], o_gn, o_gn)
    grad_inner(q, gi_own)

    def split(o, to_mate, landing):
        piece = o[...].astype(F32)
        left, right = piece[:, 0:SHARE], piece[:, SHARE:GROUP]
        own = jnp.where(first, left, right)
        to_mate[...] = jnp.where(first, right, left).astype(BF16)
        return own, send(to_mate, landing, mate)

    mirrored_wait(m_out)
    own, c_out_mate = split(o_out, c_out, d_out)
    branch_ref[keep] = own.astype(BF16)

    mirrored_wait(m_gn)
    own_gn, c_gn_mate = split(o_gn, c_gn, d_gn)
    c_go.wait_recv()
    go_own[...] += go_recv[...]
    out_go = pltpu.make_async_copy(go_own, gouter_ref, local_sem.at[2])
    out_go.start()
    c_gi.wait_recv()
    gi_own[...] += gi_recv[...]
    out_gi = pltpu.make_async_copy(gi_own, ginner_ref, local_sem.at[3])
    out_gi.start()

    c_out_mate.wait_recv()
    branch_ref[give] = d_out[...]
    c_gn_mate.wait_recv()
    unit_rows = unit[...]
    tail[0, keep] = own_gn
    tail[0, give] = d_gn[...].astype(F32)
    grad_normed = tail[0]
    grad_hat = grad_normed * gain_values
    weighted = grad_hat * unit_rows
    ggbuf[0] = jnp.broadcast_to(
        jnp.sum(grad_normed * unit_rows, axis=0, keepdims=True), (8, SHARE)
    )
    c_gg = [send(ggbuf.at[0], ggbuf.at[by], on_y(by)) for by in (1, 2, 3)]
    stat[11] = to_rows(
        jnp.sum(grad_hat, axis=1, keepdims=True), jnp.sum(weighted, axis=1, keepdims=True)
    )
    c_stat = [send(stat.at[11], stat.at[12], mate)]
    c_stat[0].wait_recv()
    stat[13] = stat[11] + stat[12]
    c_stat = [send(stat.at[13], stat.at[13 + by], on_a(by)) for by in (1, 2, 3)]
    for c in c_stat:
        c.wait_recv()
    stat[17] = stat[13] + stat[14] + stat[15] + stat[16]
    c_stat = [send(stat.at[17], stat.at[17 + by], on_b(by)) for by in (1, 2, 3)]
    for c in c_stat:
        c.wait_recv()
    sums = (stat[17] + stat[18] + stat[19] + stat[20]) * (1.0 / FEATURES)
    first_mean, second_mean = to_columns(sums)
    row_mean, total_second = to_columns(stat[10])
    inv_std = lax.rsqrt(total_second * (1.0 / FEATURES) + 1e-06)
    gtok_ref[...] = (inv_std * (grad_hat - first_mean - unit_rows * second_mean)).astype(BF16)
    for c in c_gg:
        c.wait_recv()
    ggain_ref[...] = (ggbuf[0] + ggbuf[1] + ggbuf[2] + ggbuf[3])[0:1]

    for c in started:
        c.wait_send()
    for c in (m_cot, m_tok, m_out, m_gn):
        mirrored_sent(c)
    out_go.wait()
    out_gi.wait()


def scratch():
    def buf(*shape, kind=BF16):
        return pltpu.VMEM(shape, kind)

    twice = lambda *shape, kind=BF16: [buf(*shape, kind=kind), buf(*shape, kind=kind)]
    return [
        buf(CHUNK, PAIR), buf(PAIR, CHUNK),
        buf(ROWS, SHARE, kind=F32), buf(21, 8, ROWS, kind=F32),
        buf(1, ROWS, SHARE, kind=F32), buf(4, 8, SHARE, kind=F32),
        buf(HALF, SHARE), *twice(HALF, SHARE), *twice(HALF, GROUP),
        *twice(4, 4, HALF, GROUP), *twice(4 * HALF, CHUNK),
        buf(4, HALF, PAIR, kind=F32), *twice(4, HALF, PAIR),
        *twice(2, QUARTER, PAIR), *twice(2, HALF, PAIR),
        *twice(HALF, PAIR, kind=F32),
        *twice(4, HALF, PAIR),
        *twice(4, 4, HALF, GROUP),
        *twice(2, 4, QUARTER, GROUP), *twice(2, 4, HALF, GROUP),
        *twice(4, HALF, GROUP), *twice(2, QUARTER, GROUP),
        *twice(2, HALF, GROUP), *twice(HALF, GROUP, kind=F32),
        *twice(HALF, GROUP), *twice(HALF, SHARE), *twice(HALF, SHARE),
        buf(HID, CHUNK, kind=F32), buf(HID, CHUNK, kind=F32), buf(HID, CHUNK, kind=F32),
        buf(CHUNK, HID, kind=F32), buf(CHUNK, HID, kind=F32), buf(CHUNK, HID, kind=F32),
        pltpu.SemaphoreType.DMA((COPIES,)),
        pltpu.SemaphoreType.DMA((COPIES,)),
        pltpu.SemaphoreType.DMA((4,)),
    ]


def body(tokens, norm_gain, inner_weight, outer_weight, cotangent):
    vmem, anywhere = pl.BlockSpec(memory_space=pltpu.VMEM), pl.BlockSpec(memory_space=pl.ANY)
    outs = pl.pallas_call(
        kernel,
        out_shape=[
            jax.ShapeDtypeStruct((ROWS, SHARE), BF16),
            jax.ShapeDtypeStruct((ROWS, SHARE), BF16),
            jax.ShapeDtypeStruct((1, SHARE), F32),
            jax.ShapeDtypeStruct((CHUNK, HID), F32),
            jax.ShapeDtypeStruct((HID, CHUNK), F32),
        ],
        in_specs=[vmem, vmem, anywhere, anywhere, vmem],
        out_specs=[vmem, vmem, vmem, anywhere, anywhere],
        scratch_shapes=scratch(),
        compiler_params=pltpu.CompilerParams(
            collective_id=0, has_side_effects=True, vmem_limit_bytes=60 * 1024 * 1024
        ),
        name="mlp_block",
    )(tokens, norm_gain.reshape(1, SHARE), inner_weight, outer_weight, cotangent)
    branch_out, grad_tokens, grad_gain, grad_inner, grad_outer = outs
    return (branch_out, grad_tokens, grad_gain.reshape(SHARE), grad_inner, grad_outer)


def solution(mesh):
    return jax.shard_map(
        body,
        mesh=mesh,
        in_specs=(P("row", "col"), P("col"), P("row", "col"), P("col", "row"), P("row", "col")),
        out_specs=(P("row", "col"), P("row", "col"), P("col"), P("row", "col"), P("col", "row")),
        check_vma=False,
    )
```

time: 643 us -> 167 us (0.26)
  waiting for transfers between devices: 420 us -> 0 us
  Pallas kernels: 0 us -> 150 us
  blocking collectives: 135 us -> 0 us
  matrix products: 45.5 us -> 0 us
  other arithmetic: 17.4 us -> 0 us
  between operations: 14.9 us -> 0.64 us
    reduce_scatter x3 -> x0, waiting for transfers between devices: 262 us -> none  [the longest x1 91.8 us: body(): lax.psum_scatter(contract_rows(normed, grad_pre), 'row', scatter_dimensio...]
    pallas_call x0 -> x1, Pallas kernels: none -> 150 us  [body(): pl.pallas_call(kernel, out_shape=[jax.ShapeDtypeStruct((ROWS, SHARE), BF1...]
    unnamed x1 -> x0, blocking collectives: 126 us -> none
    psum x1 -> x0, waiting for transfers between devices: 94.2 us -> none  [body(): grad_full = lax.psum(grad_partial, 'col')]
    all_gather x4 -> x0, waiting for transfers between devices: 60.5 us -> none  [the longest x1 50 us: body(): cot_full = lax.all_gather(cotangent, 'col', axis=1, tiled=True)]
    dot_general x6 -> x0, matrix products: 45.5 us -> none  [the longest x2 18.1 us: contract_rows(): lax.dot_general(left, right, (((0,), (0,)), ((), ())), preferred_element_...]
    reduce_sum x4 -> x0, other arithmetic: 15.7 us -> none  [the longest x1 7.33 us: body(): first_mean = jnp.mean(grad_hat, axis=1, keepdims=True)]
    unnamed x6 -> x9, local copies, waits for them, and re-layouts: 2.89 us -> 12.9 us
  transfers between devices with their start and end apart: 8 -> 0, of which waited for: 6 -> 0; matrix products, arithmetic and copies ran while one was open for 9% -> 0% of each run, Pallas kernels for 0% -> 0%
where the time goes in v2:
time: 167 us; the launch traced here: 165 us
  Pallas kernels  150 us (90%)
  local copies, waits for them, and re-layouts  14.1 us (8%)
    pallas_call x1, Pallas kernels, body(): pl.pallas_call(kernel, out_shape=[jax.ShapeDtypeStruct((ROWS, SHARE), BF1...  150 us
    unnamed x9, local copies, waits for them, and re-layouts  12.9 us

profile of v2, /device:TPU:1, one launch (start us, length us, event | category | flops | bytes accessed | tf_op | source)
XLA Modules:
  0.0 165.0 jit_solution(15559546030579660340)
XLA Ops:
  0.6 1.2 reshape.16.gain_ref
  1.9 1.7 %copy.10.tok_ref = bf16[384,192]{1,0:T(8,128)(2,1)} copy(bf16[384,192]{0,1:T(8,128)(2,1)} %param.5) | data formatting | bytes 294912 | tf_op args[0]
  3.6 1.7 %copy.11.cot_ref = bf16[384,192]{1,0:T(8,128)(2,1)} copy(bf16[384,192]{0,1:T(8,128)(2,1)} %param.9) | data formatting | bytes 294912 | tf_op args[4]
  5.3 150.3 %mlp_block.1 = (bf16[384,192]{1,0:T(8,128)(2,1)}, bf16[384,192]{1,0:T(8,128)(2,1)}, f32[1,192]{1,0:T(1,128)}, f32[1536,384]{1,0:T(8,128)}, f32[384,1536]{1,0:T(8,128)}) custom-call(bf16[384,192]{1,0:T(8,128)(2,1)} %copy.10.tok_ref, bf16[1,192]{1,0:T(2,128)(2,1)} %reshape.16.gain_ref, bf16[1536,384]{1,0:T(8,128)(2,1)} %w_in.1, bf16[384,1536]{1,0:T(8,128)(2,1)} %w_out.1, ...), custom_call_target="tpu_custom_call" | custom-call | tf_op jit(solution)/shard_map/mlp_block/pallas_call | solution.py:562
  155.6 1.7 %copy.12 = bf16[384,192]{0,1:T(8,128)(2,1)} copy(bf16[384,192]{1,0:T(8,128)(2,1)} %get-tuple-element.15) | data formatting | bytes 294912
  157.3 1.7 %copy.13 = bf16[384,192]{0,1:T(8,128)(2,1)} copy(bf16[384,192]{1,0:T(8,128)(2,1)} %get-tuple-element.16) | data formatting | bytes 294912
  159.0 1.2 copy.17
  160.2 0.0 copy-start
  160.2 3.4 %copy.18 = f32[1536,384]{1,0:T(8,128)} copy(f32[1536,384]{1,0:T(8,128)} %get-tuple-element.28) | data formatting | bytes 4718592
  163.6 0.0 copy-done
  163.6 1.4 copy.19
Async XLA Ops:
  160.2 3.4 %copy-start = (f32[384,1536]{1,0:T(8,128)S(1)}, f32[384,1536]{1,0:T(8,128)}, u32[]{:S(2)}) copy-start(f32[384,1536]{1,0:T(8,128)} %get-tuple-element.29) | copy-start | bytes 7077892

commit v3 on v0

v3 whole, which is shorter than its diff:
```python
import functools

import jax
import jax.numpy as jnp
from jax import lax
from jax.experimental import pallas as pl
from jax.experimental.pallas import tpu as pltpu
from jax.sharding import PartitionSpec as P

inv_sqrt_two = 0.7071067811865476
inv_sqrt_tau = 0.3989422804014327
MESH = pl.DeviceIdType.MESH
BF16 = jnp.bfloat16
F32 = jnp.float32

ROWS, SHARE = 384, 192
HALF, PART = 192, 96
GROUP, CHUNK = 384, 1536
HID, PAIR = 384, 768
FEATURES = 6144
COPIES = 260
VMEM_BYTES = 54 * 1024 * 1024
ORDER = (
    "start", "mC", "s1", "g1", "s2", "C0.own", "C1.own", "g2", "s3", "C0.near", "C0.on0",
    "mT", "C1.near", "C1.on0", "C0.far", "g3", "C0.on1", "C0.on2", "C1.far", "C1.on1",
    "C1.on2", "T0.own", "C0.on3", "T1.own", "C1.on3", "T0.near", "T0.on0", "C0.end",
    "C0.cmp", "T1.on0", "T0.far", "T0.on1", "T1.near", "T0.on2", "C1.end", "C1.cmp",
    "T0.on3", "C0.rson", "T1.far", "T1.on1", "T1.on2", "T0.end", "T0.cmp", "T1.on3",
    "C1.rson", "T1.end", "T0.rson", "T1.cmp", "act0", "gpre0", "T1.rson", "act0.on",
    "gpre0.on", "act1", "gpre1", "ms", "out0.cmp", "gn0.cmp", "mt", "act1.on", "out0.on",
    "gpre1.on", "gn0.on", "mu", "gn1.cmp", "out0.cross", "gn0.cross", "GIs", "gn1.on",
    "out1.cmp", "GOo", "out0.near", "gn1.cross", "out1.on", "gn0.near", "GOs", "gn1.near",
    "out0.end", "out1.cross", "gn0.end", "gn1.end", "out1.near", "GIo", "out1.end", "GOx",
    "spG", "fin0", "spO", "GIx", "outx", "fin1",
)
FIRST_COT, FIRST_PART = "C0", 0


def gelu_parts(hidden_pre):
    cumulative = 0.5 * (1.0 + lax.erf(hidden_pre * inv_sqrt_two))
    density = jnp.exp(-0.5 * hidden_pre * hidden_pre) * inv_sqrt_tau
    return (hidden_pre * cumulative, cumulative + hidden_pre * density)


def dot_nn(left, right):
    return jnp.dot(left, right, preferred_element_type=F32)


def dot_nt(left, right):
    return lax.dot_general(
        left, right, (((1,), (1,)), ((), ())), preferred_element_type=F32
    )


def dot_tn(left, right):
    return lax.dot_general(
        left, right, (((0,), (0,)), ((), ())), preferred_element_type=F32
    )


def turn(index, by):
    return lax.rem(index + (by % 4), 4)


def merge_moments(parts, count):
    mean = sum(p[0:1] for p in parts) * (1.0 / len(parts))
    second = sum(p[1:2] + count * (p[0:1] - mean) ** 2 for p in parts)
    return jnp.concatenate([mean, second, jnp.zeros((6, ROWS), F32)], axis=0)


def kernel(
    tok_ref, gain_ref, w_in, w_out, cot_ref,
    branch_ref, gtok_ref, ggain_ref, ginner_ref, gouter_ref,
    w1, w2, unit, stat, ggbuf, gz, gx, gy, hidden, slope, sums, ms, nat_tok, nat_cot,
    mrg_tok, mrg_cot, own_tok, own_cot, g_tok, g_cot, n_tok, n_cot,
    hf_tok, hf_cot, hb_tok, hb_cot, y1_tok, y1_cot, y2_tok, y2_cot,
    act, gpre,
    pb_out, pb_gn, r1_out, r1_gn, r2_out, r2_gn, s_out, s_gn, r3_out, r3_gn, r4_out, r4_gn,
    f_out, f_gn, o_out, o_gn, c_out, c_gn, d_out, d_gn,
    go_own, go_send, go_recv, gi_own, gi_send, gi_recv,
    send_sem, recv_sem, local_sem,
):
    y = lax.axis_index("row")
    col = lax.axis_index("col")
    z, x, q = col // 8, lax.rem(col // 2, 4), lax.rem(col, 2)
    p = 1 - q
    a0, b0 = p * x + q * z, p * z + q * x
    am, ap, a2 = turn(a0, -1), turn(a0, 1), turn(a0, 2)
    bm, bp, b2 = turn(b0, -1), turn(b0, 1), turn(b0, 2)
    ym, yp, y2 = turn(y, -1), turn(y, 1), turn(y, 2)
    first, second = q == 0, y != z

    def device(yy, zz, xx, qq):
        return (yy, zz * 8 + xx * 2 + qq)

    def on_a(by):
        return device(y, lax.rem(z + q * (by % 4), 4), lax.rem(x + p * (by % 4), 4), q)

    def on_b(by):
        return device(y, lax.rem(z + p * (by % 4), 4), lax.rem(x + q * (by % 4), 4), q)

    def on_y(by):
        return device(turn(y, by), z, x, q)

    mate = device(y, z, x, p)
    mirror = device(z, y, x, q)
    started, count = [], [0]

    def copy(src, dst, to):
        at = count[0]
        count[0] += 1
        return pltpu.make_async_remote_copy(
            src_ref=src, dst_ref=dst, send_sem=send_sem.at[at], recv_sem=recv_sem.at[at],
            device_id=to, device_id_type=MESH,
        )

    def send(src, dst, to):
        c = copy(src, dst, to)
        c.start()
        started.append(c)
        return c

    def left(c):
        c.wait_send()
        started[:] = [other for other in started if other is not c]

    def rows_of(half):
        return pl.ds(pl.multiple_of(half * HALF, HALF), HALF)

    top, bottom = pl.ds(0, PART // 2), pl.ds(PART // 2, PART // 2)

    barrier = pltpu.get_barrier_semaphore()
    others = [mate] + [on(by) for on in (on_a, on_b, on_y) for by in (1, 2, 3)]
    for other in others:
        pl.semaphore_signal(barrier, inc=1, device_id=other, device_id_type=MESH)

    @pl.when(second)
    def _():
        pl.semaphore_signal(barrier, inc=1, device_id=mirror, device_id_type=MESH)

    hid_own = pl.ds(pl.multiple_of(q * HID, HID), HID)
    local_in = pltpu.make_async_copy(w_in, w1.at[:, hid_own], local_sem.at[0])
    local_out = pltpu.make_async_copy(w_out, w2.at[hid_own], local_sem.at[1])
    local_out.start()
    local_in.start()
    nat_cot[...] = cot_ref[...].astype(F32).T.astype(BF16)

    values = tok_ref[...].astype(F32)
    own_mean = jnp.sum(values, axis=0, keepdims=True) * (1.0 / SHARE)
    own_second = jnp.sum((values - own_mean) ** 2, axis=0, keepdims=True)
    stat[0] = jnp.concatenate([own_mean, own_second, jnp.zeros((6, ROWS), F32)], axis=0)
    gz[z] = jnp.broadcast_to(gain_ref[...].astype(F32).reshape(1, SHARE), (8, SHARE))

    @pl.when(second)
    def _():
        pl.semaphore_wait(barrier, len(others) + 1)

    @pl.when(jnp.logical_not(second))
    def _():
        pl.semaphore_wait(barrier, len(others))

    def joined(own, other):
        return jnp.where(
            first,
            jnp.concatenate([own, other], axis=1),
            jnp.concatenate([other, own], axis=1),
        )

    def mirrored(piece, landing, at_home):
        c = copy(piece, landing, mirror)

        @pl.when(second)
        def _():
            c.start()

        @pl.when(jnp.logical_not(second))
        def _():
            at_home[...] = piece[...]

        return c

    def mirrored_wait(c):
        @pl.when(second)
        def _():
            c.wait_recv()

    def mirrored_sent(c):
        @pl.when(second)
        def _():
            c.wait_send()

    b_there, a_there = p * y + q * x, p * x + q * y

    class Gather:
        def __init__(self, g, part):
            self.g, self.part = g, part

        def at(self, b, a, side=None):
            rows = {None: (0, PART), 0: (0, PART // 2), 1: (PART // 2, PART // 2)}[side]
            return self.g.at[b, a, pl.ds(self.part * PART + rows[0], rows[1])]

        def own(self):
            home = self.at(b0, a0)
            self.fb = []
            self.ap, self.am = send(home, home, on_a(1)), send(home, home, on_a(-1))
            self.b = [(send(home, home, on_b(1)), send(home, home, on_b(-1)))]

        def near(self):
            self.ap.wait_recv()
            left, some = self.at(b0, am), self.at(b0, am, 0)
            self.fa_top = send(some, some, on_a(1))
            self.b.append((send(left, left, on_b(1)), send(left, left, on_b(-1))))
            self.am.wait_recv()
            right, some = self.at(b0, ap), self.at(b0, ap, 1)
            self.fa_bottom = send(some, some, on_a(-1))
            self.b.append((send(right, right, on_b(1)), send(right, right, on_b(-1))))

        def onward(self, i):
            a = (a0, am, ap, a2)[i]
            self.b[i][0].wait_recv()
            left = self.at(bm, a, 0)
            up = send(left, left, on_b(1))
            self.b[i][1].wait_recv()
            right = self.at(bp, a, 1)
            down = send(right, right, on_b(-1))
            self.fb.append((up, down))

        def far(self):
            self.fa_top.wait_recv()
            self.fa_bottom.wait_recv()
            last = self.at(b0, a2)
            self.b.append((send(last, last, on_b(1)), send(last, last, on_b(-1))))

        def end(self, n):
            for up, down in self.fb:
                up.wait_recv()
                down.wait_recv()
            rows = pl.ds(self.part * PART, PART)
            for j in range(4):
                for s in range(4):
                    to = pl.ds((self.part * 4 + j) * PART, PART)
                    n[to, s * GROUP : (s + 1) * GROUP] = self.g[p * j + q * s, p * s + q * j, rows]

    class RowSum:
        def __init__(self, hf, hb, r1, r2, part):
            self.hf, self.hb = hf.at[part], hb.at[part]
            self.r1, self.r2 = r1.at[part], r2.at[part]

        def compute(self, value):
            hf, hb, r1, r2 = self.hf, self.hb, self.r1, self.r2
            for j in range(4):
                block = value[j * PART : (j + 1) * PART]
                hf[j] = block
                hb[j] = block.astype(BF16)
            self.up1 = send(hb.at[y2, top], r1.at[0], on_y(1))
            self.down1 = send(hb.at[y2, bottom], r1.at[1], on_y(-1))
            self.up2 = send(hb.at[yp, bottom], r2.at[0, bottom], on_y(1))
            self.down2 = send(hb.at[ym, top], r2.at[1, top], on_y(-1))

        def onward(self):
            hf, hb, r1, r2 = self.hf, self.hb, self.r1, self.r2
            self.up1.wait_recv()
            hb[yp, top] = (hf[yp, top] + r1[0].astype(F32)).astype(BF16)
            self.up3 = send(hb.at[yp, top], r2.at[0, top], on_y(1))
            self.down1.wait_recv()
            hb[ym, bottom] = (hf[ym, bottom] + r1[1].astype(F32)).astype(BF16)
            self.down3 = send(hb.at[ym, bottom], r2.at[1, bottom], on_y(-1))

        def end(self):
            for c in (self.up2, self.up3, self.down2, self.down3):
                c.wait_recv()
            return self.hf[y] + self.r2[0].astype(F32) + self.r2[1].astype(F32)

    class RowGather:
        def __init__(self, g, part, block):
            g = self.g = g.at[part]
            g[y] = block
            self.up, self.down = send(g.at[y], g.at[y], on_y(1)), send(g.at[y], g.at[y], on_y(-1))

        def onward(self):
            g = self.g
            self.up.wait_recv()
            self.fup = send(g.at[ym, top], g.at[ym, top], on_y(1))
            self.down.wait_recv()
            self.fdown = send(g.at[yp, bottom], g.at[yp, bottom], on_y(-1))

        def end(self):
            self.fup.wait_recv()
            self.fdown.wait_recv()
            return self.g[...].reshape(4 * PART, PAIR)

    class PlaneSum:
        def __init__(self, pb, r1, r2, s, r3, r4, f, o, part):
            self.pb, self.r1, self.r2, self.s = pb.at[part], r1.at[part], r2.at[part], s.at[part]
            self.r3, self.r4, self.f = r3.at[part], r4.at[part], f.at[part]
            self.o = o.at[part]

        def compute(self, product):
            pb, r1, r2 = self.pb, self.r1, self.r2
            for wide in range(2):
                value = product(wide * 2 * GROUP, 2 * GROUP)
                for j in range(4):
                    for t in range(2):
                        s = wide * 2 + t
                        pb[p * j + q * s, p * s + q * j] = value[
                            j * PART : (j + 1) * PART, t * GROUP : (t + 1) * GROUP
                        ].astype(BF16)
            self.up1 = send(pb.at[b2, :, top], r1.at[0], on_b(1))
            self.down1 = send(pb.at[b2, :, bottom], r1.at[1], on_b(-1))
            self.up2 = send(pb.at[bp, :, bottom], r2.at[0, :, bottom], on_b(1))
            self.down2 = send(pb.at[bm, :, top], r2.at[1, :, top], on_b(-1))

        def onward(self):
            pb, r1, r2 = self.pb, self.r1, self.r2
            self.up1.wait_recv()
            pb[bp, :, top] = (pb[bp, :, top].astype(F32) + r1[0].astype(F32)).astype(BF16)
            self.up3 = send(pb.at[bp, :, top], r2.at[0, :, top], on_b(1))
            self.down1.wait_recv()
            pb[bm, :, bottom] = (pb[bm, :, bottom].astype(F32) + r1[1].astype(F32)).astype(BF16)
            self.down3 = send(pb.at[bm, :, bottom], r2.at[1, :, bottom], on_b(-1))

        def cross(self):
            pb, r2, s, r3, r4 = self.pb, self.r2, self.s, self.r3, self.r4
            for c in (self.up2, self.down2, self.up3, self.down3):
                c.wait_recv()

            def summed(a):
                return pb[b0, a].astype(F32) + r2[0, a].astype(F32) + r2[1, a].astype(F32)

            s[a2] = summed(a2).astype(BF16)
            self.up4 = send(s.at[a2, top], r3.at[0], on_a(1))
            self.down4 = send(s.at[a2, bottom], r3.at[1], on_a(-1))
            s[ap] = summed(ap).astype(BF16)
            self.up5 = send(s.at[ap, bottom], r4.at[0, bottom], on_a(1))
            s[am] = summed(am).astype(BF16)
            self.down5 = send(s.at[am, top], r4.at[1, top], on_a(-1))
            self.f[...] = summed(a0)

        def near(self):
            s, r3, r4 = self.s, self.r3, self.r4
            self.up4.wait_recv()
            s[ap, top] = (s[ap, top].astype(F32) + r3[0].astype(F32)).astype(BF16)
            self.up6 = send(s.at[ap, top], r4.at[0, top], on_a(1))
            self.down4.wait_recv()
            s[am, bottom] = (s[am, bottom].astype(F32) + r3[1].astype(F32)).astype(BF16)
            self.down6 = send(s.at[am, bottom], r4.at[1, bottom], on_a(-1))

        def end(self):
            for c in (self.up5, self.down5, self.up6, self.down6):
                c.wait_recv()
            total = self.f[...] + self.r4[0].astype(F32) + self.r4[1].astype(F32)
            self.s[a0] = total.astype(BF16)
            self.m = mirrored(self.s.at[a0], self.o, self.o)

    give, keep = rows_of(p), rows_of(q)
    gain_column = []
    gather = {f"C{m}": Gather(g_cot, m) for m in range(2)}
    gather |= {f"T{m}": Gather(g_tok, m) for m in range(2)}
    row_sum = {f"C{m}": RowSum(hf_cot, hb_cot, y1_cot, y2_cot, m) for m in range(2)}
    row_sum |= {f"T{m}": RowSum(hf_tok, hb_tok, y1_tok, y2_tok, m) for m in range(2)}
    row_gather, plane_sum, c = {}, {}, {}
    for m in range(2):
        plane_sum[f"out{m}"] = PlaneSum(
            pb_out, r1_out, r2_out, s_out, r3_out, r4_out, f_out, o_out, m
        )
        plane_sum[f"gn{m}"] = PlaneSum(pb_gn, r1_gn, r2_gn, s_gn, r3_gn, r4_gn, f_gn, o_gn, m)

    def three(src, buffer, first_slot, on):
        return [send(src, buffer.at[first_slot + by - 1], on(by)) for by in (1, 2, 3)]

    def arrived(copies):
        for one in copies:
            one.wait_recv()

    def on_z(by):
        return device(y, turn(z, by), x, q)

    def on_x(by):
        return device(y, z, turn(x, by), q)

    def start():
        c["mrg_cot"] = send(nat_cot.at[give], mrg_cot, mate)
        c["st0"] = send(stat.at[0], stat.at[1], mate)
        c["w2"] = send(w_out, w2.at[hid_own], mate)
        c["w1"] = send(w_in, w1.at[:, hid_own], mate)
        c["gz"] = [send(gz.at[z], gz.at[z], on_z(by)) for by in (1, 2, 3)]

    def cot_swap():
        c["mrg_cot"].wait_recv()
        own_cot[...] = joined(nat_cot[keep].astype(F32), mrg_cot[...].astype(F32)).astype(BF16)
        c["swC"] = mirrored(own_cot, g_cot.at[b_there, a_there], g_cot.at[b0, a0])

    def moments_cores():
        c["st0"].wait_recv()
        stat[2] = merge_moments([stat[0], stat[1]], SHARE)
        c["st1"] = three(stat.at[2], stat, 3, on_a)

    def moments_a():
        arrived(c["st1"])
        stat[6] = merge_moments([stat[2 + by] for by in range(4)], 2 * SHARE)
        c["st2"] = three(stat.at[6], stat, 7, on_b)

    def moments_b():
        arrived(c["st2"])
        moments = merge_moments([stat[6 + by] for by in range(4)], 8 * SHARE)
        inv_std = lax.rsqrt(moments[1:2] * (1.0 / FEATURES) + 1e-06)
        unit[...] = (tok_ref[...].astype(F32) - moments[0:1]) * inv_std
        stat[10] = jnp.broadcast_to(inv_std, (8, ROWS))
        gain_column.append(jnp.broadcast_to(gain_ref[...].astype(F32).reshape(1, SHARE), (128, SHARE)).T[:, 0:1])
        nat_tok[...] = (unit[...] * gain_column[0]).T.astype(BF16)
        c["mrg_tok"] = send(nat_tok.at[give], mrg_tok, mate)

    def tok_swap():
        c["mrg_tok"].wait_recv()
        own_tok[...] = joined(nat_tok[keep].astype(F32), mrg_tok[...].astype(F32)).astype(BF16)
        c["swT"] = mirrored(own_tok, g_tok.at[b_there, a_there], g_tok.at[b0, a0])

    def gain_z():
        arrived(c["gz"])
        c["gm"] = send(gz.at[y], gz.at[4], mate)

    def gain_cores():
        c["gm"].wait_recv()
        gx[x] = joined(gz[y], gz[4])
        c["gx"] = [send(gx.at[x], gx.at[x], on_x(by)) for by in (1, 2, 3)]

    def gain_x():
        arrived(c["gx"])
        local_in.wait()
        c["w1"].wait_recv()
        gy[0] = sum(
            dot_nn(gx[s].astype(BF16), w1[s * GROUP : (s + 1) * GROUP]) for s in range(4)
        )
        c["gy"] = three(gy.at[0], gy, 1, on_y)

    def part_rows(m):
        return pl.ds(m * 4 * PART, 4 * PART)

    def own_part(name):
        if name[1] == "0":
            mirrored_wait(c["sw" + name[0]])
        gather[name].own()

    def end_part(name):
        gather[name].end(n_cot if name[0] == "C" else n_tok)

    def compute(name):
        rows = part_rows(int(name[1]))
        if name[0] == "C":
            if name == FIRST_COT:
                local_out.wait()
                c["w2"].wait_recv()
            row_sum[name].compute(dot_nt(n_cot[rows], w2[...]))
        else:
            row_sum[name].compute(dot_nn(n_tok[rows], w1[...]))

    def gelu(m):
        hidden_pre = row_sum[f"T{m}"].end()
        gelu_value, slope[m] = gelu_parts(hidden_pre)
        hidden[m] = hidden_pre
        row_gather[f"act{m}"] = RowGather(act, m, gelu_value.astype(BF16))

    def gradient(m):
        if m == FIRST_PART:
            arrived(c["gy"])
        grad_pre = (row_sum[f"C{m}"].end() * slope[m]).astype(BF16)
        row_gather[f"gpre{m}"] = RowGather(gpre, m, grad_pre)
        grad_pre = grad_pre.astype(F32)
        gain_row = (gy[0] + gy[1] + gy[2] + gy[3])[0:1]
        one = jnp.sum(grad_pre * gain_row, axis=1, keepdims=True)
        two = jnp.sum(grad_pre * hidden[m], axis=1, keepdims=True)
        lane = lax.broadcasted_iota(jnp.int32, (PART, 128), 1)
        sums[m * PART : (m + 1) * PART] = jnp.where(lane == 0, one, two)

    def means_cores():
        ms[0] = sums[...].T[0:8]
        c["ms0"] = three(ms.at[0], ms, 1, on_a)

    def means_a():
        arrived(c["ms0"])
        ms[4] = ms[0] + ms[1] + ms[2] + ms[3]
        c["ms1"] = three(ms.at[4], ms, 5, on_b)

    def means_b():
        arrived(c["ms1"])
        ms[8] = (ms[4] + ms[5] + ms[6] + ms[7]) * (1.0 / FEATURES)
        c["ms2"] = send(ms.at[8], ms.at[9], mate)

    def out_compute(m):
        block = row_gather[f"act{m}"].end()
        plane_sum[f"out{m}"].compute(lambda at, wide: dot_nn(block, w2[:, at : at + wide]))

    def gn_compute(m):
        block = row_gather[f"gpre{m}"].end()
        plane_sum[f"gn{m}"].compute(lambda at, wide: dot_nt(block, w1[at : at + wide]))

    def by_hidden(who):
        return pl.ds(pl.multiple_of(who * HID, HID), HID)

    def grad_outer(who, into):
        block = act[:, :, :, by_hidden(who)].reshape(8 * PART, HID)
        into[...] = dot_tn(block, n_cot[...])

    def grad_inner(who, into):
        block = gpre[:, :, :, by_hidden(who)].reshape(8 * PART, HID)

        def step(t, _):
            at = pl.ds(pl.multiple_of(t * GROUP, GROUP), GROUP)
            into[at] = dot_tn(n_tok[:, at], block)
            return 0

        lax.fori_loop(0, 4, step, 0)

    def outer_send():
        grad_outer(p, go_send)
        c["go"] = send(go_send, go_recv, mate)

    def inner_send():
        grad_inner(p, gi_send)
        c["gi"] = send(gi_send, gi_recv, mate)

    def outer_add():
        c["go"].wait_recv()
        gouter_ref[...] = go_own[...] + go_recv[...]

    def inner_add():
        c["gi"].wait_recv()
        ginner_ref[...] = gi_own[...] + gi_recv[...]

    def split(name, o, to_mate, landing):
        for m in range(2):
            mirrored_wait(plane_sum[f"{name}{m}"].m)
        piece = o[...].reshape(HALF, GROUP).astype(F32)
        low, high = piece[:, 0:SHARE], piece[:, SHARE:GROUP]
        to_mate[...] = jnp.where(first, high, low).astype(BF16)
        return jnp.where(first, low, high).astype(BF16), send(to_mate, landing, mate)

    def out_split():
        left(c["mrg_cot"])
        nat_cot[keep], c["out"] = split("out", o_out, c_out, d_out)

    def gn_split():
        left(c["mrg_tok"])
        nat_tok[keep], c["gn"] = split("gn", o_gn, c_gn, d_gn)

    def out_end():
        c["out"].wait_recv()
        nat_cot[give] = d_out[...]
        branch_ref[...] = nat_cot[...].astype(F32).T.astype(BF16)

    def gn_end():
        c["gn"].wait_recv()
        nat_tok[give] = d_gn[...]
        unit_rows = unit[...]
        grad_normed = nat_tok[...].astype(F32).T
        gain_part = jnp.sum(grad_normed * unit_rows, axis=1, keepdims=True)
        ggbuf[0] = jnp.broadcast_to(gain_part, (SHARE, 128)).T[0:8]
        c["gg"] = three(ggbuf.at[0], ggbuf, 1, on_y)
        c["ms2"].wait_recv()
        means = joined(ms[8], ms[9])
        grad_hat = grad_normed * gain_column[0]
        gtok_ref[...] = (
            stat[10, 0:1] * (grad_hat - means[0:1] - unit_rows * means[1:2])
        ).astype(BF16)

    def gain_end():
        arrived(c["gg"])
        ggain_ref[...] = (ggbuf[0] + ggbuf[1] + ggbuf[2] + ggbuf[3])[0:1]

    events = {
        "start": start, "mC": cot_swap, "s1": moments_cores, "s2": moments_a, "s3": moments_b,
        "mT": tok_swap, "g1": gain_z, "g2": gain_cores, "g3": gain_x,
        "ms": means_cores, "mt": means_a, "mu": means_b,
        "GOs": outer_send, "GOo": lambda: grad_outer(q, go_own), "GOx": outer_add,
        "GIs": inner_send, "GIo": lambda: grad_inner(q, gi_own), "GIx": inner_add,
        "spO": out_split, "spG": gn_split, "outx": out_end, "fin0": gn_end, "fin1": gain_end,
    }
    for m in range(2):
        events |= {
            f"act{m}": functools.partial(gelu, m),
            f"gpre{m}": functools.partial(gradient, m),
            f"out{m}.cmp": functools.partial(out_compute, m),
            f"gn{m}.cmp": functools.partial(gn_compute, m),
        }
    steps = {}
    for name, one in gather.items():
        steps[f"{name}.own"] = functools.partial(own_part, name)
        steps[f"{name}.end"] = functools.partial(end_part, name)
        steps[f"{name}.cmp"] = functools.partial(compute, name)
        steps[f"{name}.rson"] = row_sum[name].onward
        steps[f"{name}.near"], steps[f"{name}.far"] = one.near, one.far
        for i in range(4):
            steps[f"{name}.on{i}"] = functools.partial(one.onward, i)
    for name, one in plane_sum.items():
        for step in ("on", "cross", "near", "end"):
            steps[f"{name}.{step}"] = getattr(one, {"on": "onward"}.get(step, step))
    for name in ORDER:
        if name in events:
            events.pop(name)()
        elif name.endswith(".on") and name[:-3] in row_gather:
            row_gather[name[:-3]].onward()
        else:
            steps.pop(name)()
    assert not events and not steps

    for one in started:
        one.wait_send()
    for one in (c["swC"], c["swT"], *(plane.m for plane in plane_sum.values())):
        mirrored_sent(one)


def scratch():
    def buf(*shape, kind=BF16):
        return pltpu.VMEM(shape, kind)

    def twice(*shape, kind=BF16):
        return [buf(*shape, kind=kind), buf(*shape, kind=kind)]

    return [
        buf(CHUNK, PAIR), buf(PAIR, CHUNK),
        buf(SHARE, ROWS, kind=F32), buf(11, 8, ROWS, kind=F32),
        buf(4, 8, SHARE, kind=F32),
        buf(5, 8, SHARE, kind=F32), buf(4, 8, GROUP, kind=F32), buf(4, 8, PAIR, kind=F32),
        buf(2, PART, PAIR, kind=F32), buf(2, PART, PAIR, kind=F32),
        buf(HALF, 128, kind=F32), buf(10, 8, HALF, kind=F32),
        *twice(ROWS, SHARE), *twice(HALF, SHARE), *twice(HALF, GROUP),
        *twice(4, 4, HALF, GROUP), *twice(8 * PART, CHUNK),
        *twice(2, 4, PART, PAIR, kind=F32), *twice(2, 4, PART, PAIR),
        *twice(2, 2, PART // 2, PAIR), *twice(2, 2, PART, PAIR),
        *twice(2, 4, PART, PAIR),
        *twice(2, 4, 4, PART, GROUP),
        *twice(2, 2, 4, PART // 2, GROUP), *twice(2, 2, 4, PART, GROUP),
        *twice(2, 4, PART, GROUP), *twice(2, 2, PART // 2, GROUP),
        *twice(2, 2, PART, GROUP), *twice(2, PART, GROUP, kind=F32),
        *twice(2, PART, GROUP), *twice(HALF, SHARE), *twice(HALF, SHARE),
        buf(HID, CHUNK, kind=F32), buf(HID, CHUNK, kind=F32), buf(HID, CHUNK, kind=F32),
        buf(CHUNK, HID, kind=F32), buf(CHUNK, HID, kind=F32), buf(CHUNK, HID, kind=F32),
        pltpu.SemaphoreType.DMA((COPIES,)),
        pltpu.SemaphoreType.DMA((COPIES,)),
        pltpu.SemaphoreType.DMA((2,)),
    ]


def deliver(*refs):
    sources, landings, sem = refs[:5], refs[5:10], refs[10]
    moves = [
        pltpu.make_async_copy(source, landing, sem.at[i])
        for i, (source, landing) in enumerate(zip(sources, landings))
    ]
    for move in moves:
        move.start()
    for move in moves:
        move.wait()


def body(tokens, norm_gain, inner_weight, outer_weight, cotangent):
    vmem, anywhere = pl.BlockSpec(memory_space=pltpu.VMEM), pl.BlockSpec(memory_space=pl.ANY)
    shapes = [
        ((SHARE, ROWS), BF16), ((SHARE, ROWS), BF16), ((1, SHARE), F32),
        ((CHUNK, HID), F32), ((HID, CHUNK), F32),
    ]
    outs = pl.pallas_call(
        kernel,
        out_shape=[pltpu.VMEM(shape, kind) for shape, kind in shapes],
        in_specs=[vmem, vmem, anywhere, anywhere, vmem],
        out_specs=[vmem] * 5,
        scratch_shapes=scratch(),
        compiler_params=pltpu.CompilerParams(
            collective_id=0, has_side_effects=True, vmem_limit_bytes=VMEM_BYTES
        ),
        name="mlp_block",
    )(tokens.T, norm_gain, inner_weight, outer_weight, cotangent.T)
    branch_out, grad_tokens, grad_gain, grad_inner, grad_outer = pl.pallas_call(
        deliver,
        out_shape=[jax.ShapeDtypeStruct(shape, kind) for shape, kind in shapes],
        in_specs=[vmem] * 5,
        out_specs=[anywhere] * 5,
        scratch_shapes=[pltpu.SemaphoreType.DMA((5,))],
        name="deliver",
    )(*outs)
    return (branch_out.T, grad_tokens.T, grad_gain.reshape(SHARE), grad_inner, grad_outer)


def solution(mesh):
    return jax.shard_map(
        body,
        mesh=mesh,
        in_specs=(P("row", "col"), P("col"), P("row", "col"), P("col", "row"), P("row", "col")),
        out_specs=(P("row", "col"), P("row", "col"), P("col"), P("row", "col"), P("col", "row")),
        check_vma=False,
    )
```

time: 643 us -> 137 us (0.21)
  waiting for transfers between devices: 420 us -> 0 us
  blocking collectives: 135 us -> 0 us
  Pallas kernels: 0 us -> 131 us
  matrix products: 45.5 us -> 0 us
  other arithmetic: 17.4 us -> 0 us
  between operations: 14.9 us -> 0.81 us
    reduce_scatter x3 -> x0, waiting for transfers between devices: 262 us -> none  [the longest x1 91.8 us: body(): lax.psum_scatter(contract_rows(normed, grad_pre), 'row', scatter_dimensio...]
    pallas_call x0 -> x2, Pallas kernels: none -> 131 us  [the longest x1 126 us: body(): pl.pallas_call(kernel, out_shape=[pltpu.VMEM(shape, kind) for shape, kind...]
    unnamed x1 -> x0, blocking collectives: 126 us -> none
    psum x1 -> x0, waiting for transfers between devices: 94.2 us -> none  [body(): grad_full = lax.psum(grad_partial, 'col')]
    all_gather x4 -> x0, waiting for transfers between devices: 60.5 us -> none  [the longest x1 50 us: body(): cot_full = lax.all_gather(cotangent, 'col', axis=1, tiled=True)]
    dot_general x6 -> x0, matrix products: 45.5 us -> none  [the longest x2 18.1 us: contract_rows(): lax.dot_general(left, right, (((0,), (0,)), ((), ())), preferred_element_...]
    reduce_sum x4 -> x0, other arithmetic: 15.7 us -> none  [the longest x1 7.33 us: body(): first_mean = jnp.mean(grad_hat, axis=1, keepdims=True)]
    psum x1 -> x0, blocking collectives: 8.98 us -> none  [body(): grad_gain = lax.psum(jnp.sum(grad_share * unit_share, axis=0), 'row')]
  transfers between devices with their start and end apart: 8 -> 0, of which waited for: 6 -> 0; matrix products, arithmetic and copies ran while one was open for 9% -> 0% of each run, Pallas kernels for 0% -> 0%
where the time goes in v3:
time: 137 us
  Pallas kernels  131 us (96%)
  local copies, waits for them, and re-layouts  4.69 us (3%)
    pallas_call x1, Pallas kernels, body(): pl.pallas_call(kernel, out_shape=[pltpu.VMEM(shape, kind) for shape, kind...  126 us
    pallas_call x1, Pallas kernels, body(): pl.pallas_call(deliver, out_shape=[jax.ShapeDtypeStruct(shape, kind) for...  4.84 us
    unnamed x10, local copies, waits for them, and re-layouts  4.69 us

profile of v3, /device:TPU:1, one launch (start us, length us, event | category | flops | bytes accessed | tf_op | source)
XLA Modules:
  0.0 136.8 jit_solution(689612243303561332)
XLA Ops:
  0.6 126.4 %mlp_block.1 = (bf16[192,384]{1,0:T(8,128)(2,1)S(1)}, bf16[192,384]{1,0:T(8,128)(2,1)S(1)}, f32[1,192]{1,0:T(1,128)S(1)}, f32[1536,384]{1,0:T(8,128)S(1)}, f32[384,1536]{1,0:T(8,128)S(1)}) custom-call(bf16[192,384]{1,0:T(8,128)(2,1)} %bitcast.5, bf16[192]{0:T(256)(128)(2,1)} %gain_ref.1, bf16[1536,384]{1,0:T(8,128)(2,1)} %w_in.1, bf16[384,1536]{1,0:T(8,128)(2,1)} %w_out.1, ...), custom_call_target="tpu_custom_call" | custom-call | tf_op jit(solution)/shard_map/mlp_block/pallas_call | solution.py:662
  127.1 0.0 copy-start
  127.1 1.4 %copy-done = f32[1536,384]{1,0:T(8,128)} copy-done((f32[1536,384]{1,0:T(8,128)}, f32[1536,384]{1,0:T(8,128)S(1)}, u32[]{:S(2)}) %copy-start) | copy-done | bytes 2359320
  128.5 0.0 copy-start.1
  128.5 1.4 %copy-done.1 = f32[384,1536]{1,0:T(8,128)} copy-done((f32[384,1536]{1,0:T(8,128)}, f32[384,1536]{1,0:T(8,128)S(1)}, u32[]{:S(2)}) %copy-start.1) | copy-done | bytes 2359320
  129.9 0.0 copy-start.2
  129.9 0.7 copy-done.2
  130.6 0.0 copy-start.3
  130.6 0.6 copy-done.3
  131.2 0.0 copy-start.4
  131.2 0.6 copy-done.4
  131.8 4.8 %deliver.1 = (bf16[192,384]{1,0:T(8,128)(2,1)}, bf16[192,384]{1,0:T(8,128)(2,1)}, f32[1,192]{1,0:T(1,128)}, f32[1536,384]{1,0:T(8,128)}, f32[384,1536]{1,0:T(8,128)}) custom-call(bf16[192,384]{1,0:T(8,128)(2,1)} %copy-done.2, bf16[192,384]{1,0:T(8,128)(2,1)} %copy-done.3, f32[1,192]{1,0:T(1,128)} %copy-done.4, f32[1536,384]{1,0:T(8,128)} %copy-done, ...), custom_call_target="tpu_custom_call" | custom-call | tf_op jit(solution)/shard_map/deliver/pallas_call | solution.py:673
Async XLA Ops:
  127.1 1.4 %copy-start = (f32[1536,384]{1,0:T(8,128)}, f32[1536,384]{1,0:T(8,128)S(1)}, u32[]{:S(2)}) copy-start(f32[1536,384]{1,0:T(8,128)S(1)} %get-tuple-element.18.refs_3_) | copy-start | bytes 7077892
  128.5 1.4 %copy-start.1 = (f32[384,1536]{1,0:T(8,128)}, f32[384,1536]{1,0:T(8,128)S(1)}, u32[]{:S(2)}) copy-start(f32[384,1536]{1,0:T(8,128)S(1)} %get-tuple-element.19.refs_4_) | copy-start | bytes 7077892
  129.9 0.7 copy-start.2
  130.6 0.7 copy-start.3
  131.2 0.6 copy-start.4

commit v4 on v3

--- a/solution.py
+++ b/solution.py
@@ -14,26 +14,14 @@
 F32 = jnp.float32
 
 ROWS, SHARE = 384, 192
-HALF, PART = 192, 96
+HALF, PARTS = 192, 3
+PART = HALF // PARTS
 GROUP, CHUNK = 384, 1536
 HID, PAIR = 384, 768
 FEATURES = 6144
-COPIES = 260
+COPIES = 360
 VMEM_BYTES = 54 * 1024 * 1024
-ORDER = (
-    "start", "mC", "s1", "g1", "s2", "C0.own", "C1.own", "g2", "s3", "C0.near", "C0.on0",
-    "mT", "C1.near", "C1.on0", "C0.far", "g3", "C0.on1", "C0.on2", "C1.far", "C1.on1",
-    "C1.on2", "T0.own", "C0.on3", "T1.own", "C1.on3", "T0.near", "T0.on0", "C0.end",
-    "C0.cmp", "T1.on0", "T0.far", "T0.on1", "T1.near", "T0.on2", "C1.end", "C1.cmp",
-    "T0.on3", "C0.rson", "T1.far", "T1.on1", "T1.on2", "T0.end", "T0.cmp", "T1.on3",
-    "C1.rson", "T1.end", "T0.rson", "T1.cmp", "act0", "gpre0", "T1.rson", "act0.on",
-    "gpre0.on", "act1", "gpre1", "ms", "out0.cmp", "gn0.cmp", "mt", "act1.on", "out0.on",
-    "gpre1.on", "gn0.on", "mu", "gn1.cmp", "out0.cross", "gn0.cross", "GIs", "gn1.on",
-    "out1.cmp", "GOo", "out0.near", "gn1.cross", "out1.on", "gn0.near", "GOs", "gn1.near",
-    "out0.end", "out1.cross", "gn0.end", "gn1.end", "out1.near", "GIo", "out1.end", "GOx",
-    "spG", "fin0", "spO", "GIx", "outx", "fin1",
-)
-FIRST_COT, FIRST_PART = "C0", 0
+FIRST_COT, FIRST_PART = 2, 2
 
 
 def gelu_parts(hidden_pre):
@@ -69,13 +57,13 @@
 
 
 def kernel(
-    tok_ref, gain_ref, w_in, w_out, cot_ref,
+    tok_hbm, gain_ref, w_in, w_out, cot_hbm,
     branch_ref, gtok_ref, ggain_ref, ginner_ref, gouter_ref,
-    w1, w2, unit, stat, ggbuf, gz, gx, gy, hidden, slope, sums, ms, nat_tok, nat_cot,
-    mrg_tok, mrg_cot, own_tok, own_cot, g_tok, g_cot, n_tok, n_cot,
+    tok_ref, cot_ref, w1, w2, unit, stat, ggbuf, gz, gx, gy, hidden, slope, sums, ms, nat_tok, nat_cot,
+    mrg_tok, mrg_cot, own_tok, own_cot, raw_tok, g_tok, g_cot, n_tok, n_cot,
     hf_tok, hf_cot, hb_tok, hb_cot, y1_tok, y1_cot, y2_tok, y2_cot,
     act, gpre,
-    pb_out, pb_gn, r1_out, r1_gn, r2_out, r2_gn, s_out, s_gn, r3_out, r3_gn, r4_out, r4_gn,
+    pb_out, pb_gn, r1_out, r1_gn, r2_out, r2_gn, s_out, s_gn, r4_out, r4_gn,
     f_out, f_gn, o_out, o_gn, c_out, c_gn, d_out, d_gn,
     go_own, go_send, go_recv, gi_own, gi_send, gi_recv,
     send_sem, recv_sem, local_sem,
@@ -141,9 +129,16 @@
     hid_own = pl.ds(pl.multiple_of(q * HID, HID), HID)
     local_in = pltpu.make_async_copy(w_in, w1.at[:, hid_own], local_sem.at[0])
     local_out = pltpu.make_async_copy(w_out, w2.at[hid_own], local_sem.at[1])
+    local_tok = pltpu.make_async_copy(tok_hbm, tok_ref, local_sem.at[2])
+    local_cot = pltpu.make_async_copy(cot_hbm, cot_ref, local_sem.at[3])
+    local_cot.start()
+    local_tok.start()
     local_out.start()
     local_in.start()
+    local_cot.wait()
     nat_cot[...] = cot_ref[...].astype(F32).T.astype(BF16)
+    local_tok.wait()
+    nat_tok[...] = tok_ref[...].astype(F32).T.astype(BF16)
 
     values = tok_ref[...].astype(F32)
     own_mean = jnp.sum(values, axis=0, keepdims=True) * (1.0 / SHARE)
@@ -201,19 +196,21 @@
 
         def own(self):
             home = self.at(b0, a0)
-            self.fb = []
-            self.ap, self.am = send(home, home, on_a(1)), send(home, home, on_a(-1))
-            self.b = [(send(home, home, on_b(1)), send(home, home, on_b(-1)))]
+            self.a = [send(home, home, on_a(by)) for by in (1, -1, 2)]
+            self.b, self.fb = {0: self.both(home)}, []
+
+        def both(self, piece):
+            return send(piece, piece, on_b(1)), send(piece, piece, on_b(-1))
 
         def near(self):
-            self.ap.wait_recv()
-            left, some = self.at(b0, am), self.at(b0, am, 0)
-            self.fa_top = send(some, some, on_a(1))
-            self.b.append((send(left, left, on_b(1)), send(left, left, on_b(-1))))
-            self.am.wait_recv()
-            right, some = self.at(b0, ap), self.at(b0, ap, 1)
-            self.fa_bottom = send(some, some, on_a(-1))
-            self.b.append((send(right, right, on_b(1)), send(right, right, on_b(-1))))
+            self.a[0].wait_recv()
+            self.b[1] = self.both(self.at(b0, am))
+            self.a[1].wait_recv()
+            self.b[2] = self.both(self.at(b0, ap))
+
+        def far(self):
+            self.a[2].wait_recv()
+            self.b[3] = self.both(self.at(b0, a2))
 
         def onward(self, i):
             a = (a0, am, ap, a2)[i]
@@ -224,12 +221,6 @@
             right = self.at(bp, a, 1)
             down = send(right, right, on_b(-1))
             self.fb.append((up, down))
-
-        def far(self):
-            self.fa_top.wait_recv()
-            self.fa_bottom.wait_recv()
-            last = self.at(b0, a2)
-            self.b.append((send(last, last, on_b(1)), send(last, last, on_b(-1))))
 
         def end(self, n):
             for up, down in self.fb:
@@ -290,10 +281,9 @@
             return self.g[...].reshape(4 * PART, PAIR)
 
     class PlaneSum:
-        def __init__(self, pb, r1, r2, s, r3, r4, f, o, part):
+        def __init__(self, pb, r1, r2, s, r4, f, o, part):
             self.pb, self.r1, self.r2, self.s = pb.at[part], r1.at[part], r2.at[part], s.at[part]
-            self.r3, self.r4, self.f = r3.at[part], r4.at[part], f.at[part]
-            self.o = o.at[part]
+            self.r4, self.f, self.o = r4.at[part], f.at[part], o.at[part]
 
         def compute(self, product):
             pb, r1, r2 = self.pb, self.r1, self.r2
@@ -320,50 +310,37 @@
             self.down3 = send(pb.at[bm, :, bottom], r2.at[1, :, bottom], on_b(-1))
 
         def cross(self):
-            pb, r2, s, r3, r4 = self.pb, self.r2, self.s, self.r3, self.r4
+            pb, r2, s, r4 = self.pb, self.r2, self.s, self.r4
             for c in (self.up2, self.down2, self.up3, self.down3):
                 c.wait_recv()
 
             def summed(a):
                 return pb[b0, a].astype(F32) + r2[0, a].astype(F32) + r2[1, a].astype(F32)
 
-            s[a2] = summed(a2).astype(BF16)
-            self.up4 = send(s.at[a2, top], r3.at[0], on_a(1))
-            self.down4 = send(s.at[a2, bottom], r3.at[1], on_a(-1))
-            s[ap] = summed(ap).astype(BF16)
-            self.up5 = send(s.at[ap, bottom], r4.at[0, bottom], on_a(1))
-            s[am] = summed(am).astype(BF16)
-            self.down5 = send(s.at[am, top], r4.at[1, top], on_a(-1))
+            self.a = []
+            for slot, (to, by) in enumerate(((a2, 2), (ap, 1), (am, -1))):
+                s[to] = summed(to).astype(BF16)
+                self.a.append(send(s.at[to], r4.at[slot], on_a(by)))
             self.f[...] = summed(a0)
 
-        def near(self):
-            s, r3, r4 = self.s, self.r3, self.r4
-            self.up4.wait_recv()
-            s[ap, top] = (s[ap, top].astype(F32) + r3[0].astype(F32)).astype(BF16)
-            self.up6 = send(s.at[ap, top], r4.at[0, top], on_a(1))
-            self.down4.wait_recv()
-            s[am, bottom] = (s[am, bottom].astype(F32) + r3[1].astype(F32)).astype(BF16)
-            self.down6 = send(s.at[am, bottom], r4.at[1, bottom], on_a(-1))
-
         def end(self):
-            for c in (self.up5, self.down5, self.up6, self.down6):
+            for c in self.a:
                 c.wait_recv()
-            total = self.f[...] + self.r4[0].astype(F32) + self.r4[1].astype(F32)
+            total = self.f[...] + sum(self.r4[slot].astype(F32) for slot in range(3))
             self.s[a0] = total.astype(BF16)
             self.m = mirrored(self.s.at[a0], self.o, self.o)
 
     give, keep = rows_of(p), rows_of(q)
-    gain_column = []
-    gather = {f"C{m}": Gather(g_cot, m) for m in range(2)}
-    gather |= {f"T{m}": Gather(g_tok, m) for m in range(2)}
-    row_sum = {f"C{m}": RowSum(hf_cot, hb_cot, y1_cot, y2_cot, m) for m in range(2)}
-    row_sum |= {f"T{m}": RowSum(hf_tok, hb_tok, y1_tok, y2_tok, m) for m in range(2)}
-    row_gather, plane_sum, c = {}, {}, {}
-    for m in range(2):
-        plane_sum[f"out{m}"] = PlaneSum(
-            pb_out, r1_out, r2_out, s_out, r3_out, r4_out, f_out, o_out, m
-        )
-        plane_sum[f"gn{m}"] = PlaneSum(pb_gn, r1_gn, r2_gn, s_gn, r3_gn, r4_gn, f_gn, o_gn, m)
+    gain_column, moment_columns = [], []
+    cot = [Gather(g_cot, m) for m in range(PARTS)]
+    tok = [Gather(g_tok, m) for m in range(PARTS)]
+    cot_sum = [RowSum(hf_cot, hb_cot, y1_cot, y2_cot, m) for m in range(PARTS)]
+    tok_sum = [RowSum(hf_tok, hb_tok, y1_tok, y2_tok, m) for m in range(PARTS)]
+    out_sum = [
+        PlaneSum(pb_out, r1_out, r2_out, s_out, r4_out, f_out, o_out, m) for m in range(PARTS)
+    ]
+    gn_sum = [PlaneSum(pb_gn, r1_gn, r2_gn, s_gn, r4_gn, f_gn, o_gn, m) for m in range(PARTS)]
+    cot_swaps, tok_swaps, act_gather, gpre_gather, c = {}, {}, {}, {}, {}
 
     def three(src, buffer, first_slot, on):
         return [send(src, buffer.at[first_slot + by - 1], on(by)) for by in (1, 2, 3)]
@@ -380,15 +357,20 @@
 
     def start():
         c["mrg_cot"] = send(nat_cot.at[give], mrg_cot, mate)
+        c["mrg_tok"] = send(nat_tok.at[give], mrg_tok, mate)
         c["st0"] = send(stat.at[0], stat.at[1], mate)
         c["w2"] = send(w_out, w2.at[hid_own], mate)
         c["w1"] = send(w_in, w1.at[:, hid_own], mate)
         c["gz"] = [send(gz.at[z], gz.at[z], on_z(by)) for by in (1, 2, 3)]
 
-    def cot_swap():
+    def cot_merge():
         c["mrg_cot"].wait_recv()
         own_cot[...] = joined(nat_cot[keep].astype(F32), mrg_cot[...].astype(F32)).astype(BF16)
-        c["swC"] = mirrored(own_cot, g_cot.at[b_there, a_there], g_cot.at[b0, a0])
+
+    def cot_swap(m):
+        rows = pl.ds(m * PART, PART)
+        there, here = g_cot.at[b_there, a_there, rows], g_cot.at[b0, a0, rows]
+        cot_swaps[m] = mirrored(own_cot.at[rows], there, here)
 
     def moments_cores():
         c["st0"].wait_recv()
@@ -404,16 +386,32 @@
         arrived(c["st2"])
         moments = merge_moments([stat[6 + by] for by in range(4)], 8 * SHARE)
         inv_std = lax.rsqrt(moments[1:2] * (1.0 / FEATURES) + 1e-06)
-        unit[...] = (tok_ref[...].astype(F32) - moments[0:1]) * inv_std
-        stat[10] = jnp.broadcast_to(inv_std, (8, ROWS))
-        gain_column.append(jnp.broadcast_to(gain_ref[...].astype(F32).reshape(1, SHARE), (128, SHARE)).T[:, 0:1])
-        nat_tok[...] = (unit[...] * gain_column[0]).T.astype(BF16)
-        c["mrg_tok"] = send(nat_tok.at[give], mrg_tok, mate)
-
-    def tok_swap():
+        stat[10] = jnp.concatenate([moments[0:1], inv_std, jnp.zeros((6, ROWS), F32)], axis=0)
+        c["stM"] = mirrored(stat.at[10], stat.at[11], stat.at[11])
+
+    def own_unit():
+        unit[...] = (tok_ref[...].astype(F32) - stat[10, 0:1]) * stat[10, 1:2]
+        gain_values = gain_ref[...].astype(F32).reshape(1, SHARE)
+        gain_column.append(jnp.broadcast_to(gain_values, (128, SHARE)).T[:, 0:1])
+
+    def tok_merge():
         c["mrg_tok"].wait_recv()
         own_tok[...] = joined(nat_tok[keep].astype(F32), mrg_tok[...].astype(F32)).astype(BF16)
-        c["swT"] = mirrored(own_tok, g_tok.at[b_there, a_there], g_tok.at[b0, a0])
+
+    def tok_swap(m):
+        rows = pl.ds(m * PART, PART)
+        tok_swaps[m] = mirrored(own_tok.at[rows], raw_tok.at[rows], raw_tok.at[rows])
+
+    def normalise(m):
+        if not moment_columns:
+            mirrored_wait(c["stM"])
+            both = jnp.where(first, stat[11, :, 0:HALF], stat[11, :, HALF:ROWS])
+            both = jnp.concatenate([both, jnp.zeros((120, HALF), F32)], axis=0).T
+            moment_columns.extend([both[:, 0:1], both[:, 1:2]])
+        rows = slice(m * PART, (m + 1) * PART)
+        mean, inv_std = (column[rows] for column in moment_columns)
+        unit_rows = (raw_tok[rows].astype(F32) - mean) * inv_std
+        g_tok[b0, a0, rows] = (unit_rows * gx[x, 0:1]).astype(BF16)
 
     def gain_z():
         arrived(c["gz"])
@@ -436,35 +434,35 @@
     def part_rows(m):
         return pl.ds(m * 4 * PART, 4 * PART)
 
-    def own_part(name):
-        if name[1] == "0":
-            mirrored_wait(c["sw" + name[0]])
-        gather[name].own()
-
-    def end_part(name):
-        gather[name].end(n_cot if name[0] == "C" else n_tok)
-
-    def compute(name):
-        rows = part_rows(int(name[1]))
-        if name[0] == "C":
-            if name == FIRST_COT:
-                local_out.wait()
-                c["w2"].wait_recv()
-            row_sum[name].compute(dot_nt(n_cot[rows], w2[...]))
-        else:
-            row_sum[name].compute(dot_nn(n_tok[rows], w1[...]))
+    def cot_own(m):
+        mirrored_wait(cot_swaps[m])
+        cot[m].own()
+
+    def tok_own(m):
+        mirrored_wait(tok_swaps[m])
+        normalise(m)
+        tok[m].own()
+
+    def cot_compute(m):
+        if m == FIRST_COT:
+            local_out.wait()
+            c["w2"].wait_recv()
+        cot_sum[m].compute(dot_nt(n_cot[part_rows(m)], w2[...]))
+
+    def tok_compute(m):
+        tok_sum[m].compute(dot_nn(n_tok[part_rows(m)], w1[...]))
 
     def gelu(m):
-        hidden_pre = row_sum[f"T{m}"].end()
+        hidden_pre = tok_sum[m].end()
         gelu_value, slope[m] = gelu_parts(hidden_pre)
         hidden[m] = hidden_pre
-        row_gather[f"act{m}"] = RowGather(act, m, gelu_value.astype(BF16))
+        act_gather[m] = RowGather(act, m, gelu_value.astype(BF16))
 
     def gradient(m):
         if m == FIRST_PART:
             arrived(c["gy"])
-        grad_pre = (row_sum[f"C{m}"].end() * slope[m]).astype(BF16)
-        row_gather[f"gpre{m}"] = RowGather(gpre, m, grad_pre)
+        grad_pre = (cot_sum[m].end() * slope[m]).astype(BF16)
+        gpre_gather[m] = RowGather(gpre, m, grad_pre)
         grad_pre = grad_pre.astype(F32)
         gain_row = (gy[0] + gy[1] + gy[2] + gy[3])[0:1]
         one = jnp.sum(grad_pre * gain_row, axis=1, keepdims=True)
@@ -487,22 +485,22 @@
         c["ms2"] = send(ms.at[8], ms.at[9], mate)
 
     def out_compute(m):
-        block = row_gather[f"act{m}"].end()
-        plane_sum[f"out{m}"].compute(lambda at, wide: dot_nn(block, w2[:, at : at + wide]))
+        block = act_gather[m].end()
+        out_sum[m].compute(lambda at, wide: dot_nn(block, w2[:, at : at + wide]))
 
     def gn_compute(m):
-        block = row_gather[f"gpre{m}"].end()
-        plane_sum[f"gn{m}"].compute(lambda at, wide: dot_nt(block, w1[at : at + wide]))
+        block = gpre_gather[m].end()
+        gn_sum[m].compute(lambda at, wide: dot_nt(block, w1[at : at + wide]))
 
     def by_hidden(who):
         return pl.ds(pl.multiple_of(who * HID, HID), HID)
 
     def grad_outer(who, into):
-        block = act[:, :, :, by_hidden(who)].reshape(8 * PART, HID)
+        block = act[:, :, :, by_hidden(who)].reshape(4 * HALF, HID)
         into[...] = dot_tn(block, n_cot[...])
 
     def grad_inner(who, into):
-        block = gpre[:, :, :, by_hidden(who)].reshape(8 * PART, HID)
+        block = gpre[:, :, :, by_hidden(who)].reshape(4 * HALF, HID)
 
         def step(t, _):
             at = pl.ds(pl.multiple_of(t * GROUP, GROUP), GROUP)
@@ -527,9 +525,9 @@
         c["gi"].wait_recv()
         ginner_ref[...] = gi_own[...] + gi_recv[...]
 
-    def split(name, o, to_mate, landing):
-        for m in range(2):
-            mirrored_wait(plane_sum[f"{name}{m}"].m)
+    def split(sums, o, to_mate, landing):
+        for one in sums:
+            mirrored_wait(one.m)
         piece = o[...].reshape(HALF, GROUP).astype(F32)
         low, high = piece[:, 0:SHARE], piece[:, SHARE:GROUP]
         to_mate[...] = jnp.where(first, high, low).astype(BF16)
@@ -537,11 +535,11 @@
 
     def out_split():
         left(c["mrg_cot"])
-        nat_cot[keep], c["out"] = split("out", o_out, c_out, d_out)
+        nat_cot[keep], c["out"] = split(out_sum, o_out, c_out, d_out)
 
     def gn_split():
         left(c["mrg_tok"])
-        nat_tok[keep], c["gn"] = split("gn", o_gn, c_gn, d_gn)
+        nat_tok[keep], c["gn"] = split(gn_sum, o_gn, c_gn, d_gn)
 
     def out_end():
         c["out"].wait_recv()
@@ -560,52 +558,144 @@
         means = joined(ms[8], ms[9])
         grad_hat = grad_normed * gain_column[0]
         gtok_ref[...] = (
-            stat[10, 0:1] * (grad_hat - means[0:1] - unit_rows * means[1:2])
+            stat[10, 1:2] * (grad_hat - means[0:1] - unit_rows * means[1:2])
         ).astype(BF16)
 
     def gain_end():
         arrived(c["gg"])
         ggain_ref[...] = (ggbuf[0] + ggbuf[1] + ggbuf[2] + ggbuf[3])[0:1]
 
-    events = {
-        "start": start, "mC": cot_swap, "s1": moments_cores, "s2": moments_a, "s3": moments_b,
-        "mT": tok_swap, "g1": gain_z, "g2": gain_cores, "g3": gain_x,
-        "ms": means_cores, "mt": means_a, "mu": means_b,
-        "GOs": outer_send, "GOo": lambda: grad_outer(q, go_own), "GOx": outer_add,
-        "GIs": inner_send, "GIo": lambda: grad_inner(q, gi_own), "GIx": inner_add,
-        "spO": out_split, "spG": gn_split, "outx": out_end, "fin0": gn_end, "fin1": gain_end,
-    }
-    for m in range(2):
-        events |= {
-            f"act{m}": functools.partial(gelu, m),
-            f"gpre{m}": functools.partial(gradient, m),
-            f"out{m}.cmp": functools.partial(out_compute, m),
-            f"gn{m}.cmp": functools.partial(gn_compute, m),
-        }
-    steps = {}
-    for name, one in gather.items():
-        steps[f"{name}.own"] = functools.partial(own_part, name)
-        steps[f"{name}.end"] = functools.partial(end_part, name)
-        steps[f"{name}.cmp"] = functools.partial(compute, name)
-        steps[f"{name}.rson"] = row_sum[name].onward
-        steps[f"{name}.near"], steps[f"{name}.far"] = one.near, one.far
-        for i in range(4):
-            steps[f"{name}.on{i}"] = functools.partial(one.onward, i)
-    for name, one in plane_sum.items():
-        for step in ("on", "cross", "near", "end"):
-            steps[f"{name}.{step}"] = getattr(one, {"on": "onward"}.get(step, step))
-    for name in ORDER:
-        if name in events:
-            events.pop(name)()
-        elif name.endswith(".on") and name[:-3] in row_gather:
-            row_gather[name[:-3]].onward()
-        else:
-            steps.pop(name)()
-    assert not events and not steps
+    start()
+    cot_merge()
+    cot_swap(2)
+    cot_swap(0)
+    cot_swap(1)
+    gain_z()
+    moments_cores()
+    tok_merge()
+    tok_swap(2)
+    tok_swap(1)
+    tok_swap(0)
+    moments_a()
+    cot_own(2)
+    gain_cores()
+    cot_own(0)
+    moments_b()
+    cot[2].near()
+    own_unit()
+    cot[2].far()
+    cot[2].onward(0)
+    gain_x()
+    cot[0].near()
+    cot[0].onward(0)
+    cot[0].far()
+    cot[2].onward(1)
+    cot[2].onward(2)
+    cot[2].onward(3)
+    tok_own(2)
+    cot[0].onward(1)
+    cot[0].onward(2)
+    cot[0].onward(3)
+    tok_own(0)
+    cot[2].end(n_cot)
+    cot_compute(2)
+    tok[2].far()
+    tok[2].near()
+    tok[2].onward(0)
+    cot[0].end(n_cot)
+    cot_compute(0)
+    tok[0].near()
+    tok[0].far()
+    tok[0].onward(0)
+    cot_sum[2].onward()
+    tok[2].onward(3)
+    tok[2].onward(1)
+    tok[2].onward(2)
+    tok[0].onward(1)
+    cot_sum[0].onward()
+    tok[0].onward(2)
+    tok[0].onward(3)
+    tok[2].end(n_tok)
+    tok_compute(2)
+    tok[0].end(n_tok)
+    tok_compute(0)
+    cot_own(1)
+    tok_sum[2].onward()
+    tok_own(1)
+    cot[1].near()
+    tok_sum[0].onward()
+    gelu(2)
+    gradient(2)
+    cot[1].onward(0)
+    tok[1].near()
+    tok[1].far()
+    tok[1].onward(0)
+    cot[1].onward(1)
+    cot[1].onward(2)
+    gelu(0)
+    gradient(0)
+    cot[1].far()
+    act_gather[2].onward()
+    tok[1].onward(1)
+    tok[1].onward(2)
+    tok[1].onward(3)
+    cot[1].onward(3)
+    gpre_gather[2].onward()
+    tok[1].end(n_tok)
+    tok_compute(1)
+    act_gather[0].onward()
+    cot[1].end(n_cot)
+    cot_compute(1)
+    gpre_gather[0].onward()
+    out_compute(2)
+    gn_compute(2)
+    tok_sum[1].onward()
+    out_compute(0)
+    cot_sum[1].onward()
+    out_sum[2].onward()
+    gn_compute(0)
+    gelu(1)
+    out_sum[0].onward()
+    gradient(1)
+    means_cores()
+    out_sum[2].cross()
+    gn_sum[0].onward()
+    gn_sum[2].onward()
+    act_gather[1].onward()
+    out_sum[0].cross()
+    out_sum[2].end()
+    gpre_gather[1].onward()
+    gn_sum[0].cross()
+    gn_sum[2].cross()
+    out_compute(1)
+    gn_compute(1)
+    out_sum[0].end()
+    gn_sum[0].end()
+    outer_send()
+    gn_sum[1].onward()
+    gn_sum[2].end()
+    out_sum[1].onward()
+    inner_send()
+    gn_sum[1].cross()
+    grad_inner(q, gi_own)
+    out_sum[1].cross()
+    gn_sum[1].end()
+    means_a()
+    grad_outer(q, go_own)
+    out_sum[1].end()
+    outer_add()
+    means_b()
+    gn_split()
+    gn_end()
+    out_split()
+    inner_add()
+    out_end()
+    gain_end()
 
     for one in started:
         one.wait_send()
-    for one in (c["swC"], c["swT"], *(plane.m for plane in plane_sum.values())):
+    swaps = [*cot_swaps.values(), *tok_swaps.values(), c["stM"]]
+    for one in (*swaps, *(plane.m for plane in out_sum + gn_sum)):
         mirrored_sent(one)
 
 
@@ -617,40 +707,28 @@
         return [buf(*shape, kind=kind), buf(*shape, kind=kind)]
 
     return [
-        buf(CHUNK, PAIR), buf(PAIR, CHUNK),
-        buf(SHARE, ROWS, kind=F32), buf(11, 8, ROWS, kind=F32),
+        *twice(SHARE, ROWS), buf(CHUNK, PAIR), buf(PAIR, CHUNK),
+        buf(SHARE, ROWS, kind=F32), buf(12, 8, ROWS, kind=F32),
         buf(4, 8, SHARE, kind=F32),
         buf(5, 8, SHARE, kind=F32), buf(4, 8, GROUP, kind=F32), buf(4, 8, PAIR, kind=F32),
-        buf(2, PART, PAIR, kind=F32), buf(2, PART, PAIR, kind=F32),
+        buf(PARTS, PART, PAIR, kind=F32), buf(PARTS, PART, PAIR, kind=F32),
         buf(HALF, 128, kind=F32), buf(10, 8, HALF, kind=F32),
-        *twice(ROWS, SHARE), *twice(HALF, SHARE), *twice(HALF, GROUP),
-        *twice(4, 4, HALF, GROUP), *twice(8 * PART, CHUNK),
-        *twice(2, 4, PART, PAIR, kind=F32), *twice(2, 4, PART, PAIR),
-        *twice(2, 2, PART // 2, PAIR), *twice(2, 2, PART, PAIR),
-        *twice(2, 4, PART, PAIR),
-        *twice(2, 4, 4, PART, GROUP),
-        *twice(2, 2, 4, PART // 2, GROUP), *twice(2, 2, 4, PART, GROUP),
-        *twice(2, 4, PART, GROUP), *twice(2, 2, PART // 2, GROUP),
-        *twice(2, 2, PART, GROUP), *twice(2, PART, GROUP, kind=F32),
-        *twice(2, PART, GROUP), *twice(HALF, SHARE), *twice(HALF, SHARE),
+        *twice(ROWS, SHARE), *twice(HALF, SHARE), *twice(HALF, GROUP), buf(HALF, GROUP),
+        *twice(4, 4, HALF, GROUP), *twice(4 * HALF, CHUNK),
+        *twice(PARTS, 4, PART, PAIR, kind=F32), *twice(PARTS, 4, PART, PAIR),
+        *twice(PARTS, 2, PART // 2, PAIR), *twice(PARTS, 2, PART, PAIR),
+        *twice(PARTS, 4, PART, PAIR),
+        *twice(PARTS, 4, 4, PART, GROUP),
+        *twice(PARTS, 2, 4, PART // 2, GROUP), *twice(PARTS, 2, 4, PART, GROUP),
+        *twice(PARTS, 4, PART, GROUP), *twice(PARTS, 3, PART, GROUP),
+        *twice(PARTS, PART, GROUP, kind=F32),
+        *twice(PARTS, PART, GROUP), *twice(HALF, SHARE), *twice(HALF, SHARE),
         buf(HID, CHUNK, kind=F32), buf(HID, CHUNK, kind=F32), buf(HID, CHUNK, kind=F32),
         buf(CHUNK, HID, kind=F32), buf(CHUNK, HID, kind=F32), buf(CHUNK, HID, kind=F32),
         pltpu.SemaphoreType.DMA((COPIES,)),
         pltpu.SemaphoreType.DMA((COPIES,)),
-        pltpu.SemaphoreType.DMA((2,)),
+        pltpu.SemaphoreType.DMA((4,)),
     ]
-
-
-def deliver(*refs):
-    sources, landings, sem = refs[:5], refs[5:10], refs[10]
-    moves = [
-        pltpu.make_async_copy(source, landing, sem.at[i])
-        for i, (source, landing) in enumerate(zip(sources, landings))
-    ]
-    for move in moves:
-        move.start()
-    for move in moves:
-        move.wait()
 
 
 def body(tokens, norm_gain, inner_weight, outer_weight, cotangent):
@@ -659,10 +737,10 @@
         ((SHARE, ROWS), BF16), ((SHARE, ROWS), BF16), ((1, SHARE), F32),
         ((CHUNK, HID), F32), ((HID, CHUNK), F32),
     ]
-    outs = pl.pallas_call(
+    branch_out, grad_tokens, grad_gain, grad_inner, grad_outer = pl.pallas_call(
         kernel,
         out_shape=[pltpu.VMEM(shape, kind) for shape, kind in shapes],
-        in_specs=[vmem, vmem, anywhere, anywhere, vmem],
+        in_specs=[anywhere, vmem, anywhere, anywhere, anywhere],
         out_specs=[vmem] * 5,
         scratch_shapes=scratch(),
         compiler_params=pltpu.CompilerParams(
@@ -670,14 +748,6 @@
         ),
         name="mlp_block",
     )(tokens.T, norm_gain, inner_weight, outer_weight, cotangent.T)
-    branch_out, grad_tokens, grad_gain, grad_inner, grad_outer = pl.pallas_call(
-        deliver,
-        out_shape=[jax.ShapeDtypeStruct(shape, kind) for shape, kind in shapes],
-        in_specs=[vmem] * 5,
-        out_specs=[anywhere] * 5,
-        scratch_shapes=[pltpu.SemaphoreType.DMA((5,))],
-        name="deliver",
-    )(*outs)
     return (branch_out.T, grad_tokens.T, grad_gain.reshape(SHARE), grad_inner, grad_outer)
 
 

time: 137 us -> 129 us (0.942)
  Pallas kernels: 131 us -> 124 us
    pallas_call x1 -> x0, Pallas kernels: 4.84 us -> none  [body(): pl.pallas_call(deliver, out_shape=[jax.ShapeDtypeStruct(shape, kind) for...]
    pallas_call x1, Pallas kernels: 126 us -> 124 us  [body(): pl.pallas_call(kernel, out_shape=[pltpu.VMEM(shape, kind) for shape, kind...]
    unnamed x10 -> x5, local copies, waits for them, and re-layouts: 4.69 us -> 4.7 us
where the time goes in v4:
time: 129 us
  Pallas kernels  124 us (96%)
  local copies, waits for them, and re-layouts  4.7 us (4%)
    pallas_call x1, Pallas kernels, body(): pl.pallas_call(kernel, out_shape=[pltpu.VMEM(shape, kind) for shape, kind...  124 us
    unnamed x5, local copies, waits for them, and re-layouts  4.7 us

profile of v4, /device:TPU:1, one launch (start us, length us, event | category | flops | bytes accessed | tf_op | source)
XLA Modules:
  0.0 129.0 jit_solution(4795528109332926632)
XLA Ops:
  0.6 123.6 %mlp_block.1 = (bf16[192,384]{1,0:T(8,128)(2,1)S(1)}, bf16[192,384]{1,0:T(8,128)(2,1)S(1)}, f32[1,192]{1,0:T(1,128)S(1)}, f32[1536,384]{1,0:T(8,128)S(1)}, f32[384,1536]{1,0:T(8,128)S(1)}) custom-call(bf16[192,384]{1,0:T(8,128)(2,1)} %bitcast.8, bf16[192]{0:T(256)(128)(2,1)} %gain_ref.1, bf16[1536,384]{1,0:T(8,128)(2,1)} %w_in.1, bf16[384,1536]{1,0:T(8,128)(2,1)} %w_out.1, ...), custom_call_target="tpu_custom_call" | custom-call | tf_op jit(solution)/shard_map/mlp_block/pallas_call | solution.py:740
  124.3 0.7 copy.15
  124.9 0.7 copy.16
  125.6 0.6 copy.17
  126.2 1.4 %copy.18 = f32[1536,384]{1,0:T(8,128)} copy(f32[1536,384]{1,0:T(8,128)S(1)} %get-tuple-element.18) | data formatting | bytes 4718592
  127.6 1.4 %copy.19 = f32[384,1536]{1,0:T(8,128)} copy(f32[384,1536]{1,0:T(8,128)S(1)} %get-tuple-element.19) | data formatting | bytes 4718592

commit v5 on v4

--- a/solution.py
+++ b/solution.py
@@ -683,13 +683,13 @@
     means_a()
     grad_outer(q, go_own)
     out_sum[1].end()
-    outer_add()
     means_b()
     gn_split()
     gn_end()
     out_split()
     inner_add()
     out_end()
+    outer_add()
     gain_end()
 
     for one in started:

time: 129 us -> 129 us (level)
  no operation moved by 1% of the time
where the time goes in v5:
time: 129 us
  Pallas kernels  124 us (96%)
  local copies, waits for them, and re-layouts  4.7 us (4%)
    pallas_call x1, Pallas kernels, body(): pl.pallas_call(kernel, out_shape=[pltpu.VMEM(shape, kind) for shape, kind...  124 us
    unnamed x5, local copies, waits for them, and re-layouts  4.7 us

profile of v5, /device:TPU:1, one launch (start us, length us, event | category | flops | bytes accessed | tf_op | source)
XLA Modules:
  0.0 129.0 jit_solution(12375930802131135417)
XLA Ops:
  0.6 123.6 %mlp_block.1 = (bf16[192,384]{1,0:T(8,128)(2,1)S(1)}, bf16[192,384]{1,0:T(8,128)(2,1)S(1)}, f32[1,192]{1,0:T(1,128)S(1)}, f32[1536,384]{1,0:T(8,128)S(1)}, f32[384,1536]{1,0:T(8,128)S(1)}) custom-call(bf16[192,384]{1,0:T(8,128)(2,1)} %bitcast.8, bf16[192]{0:T(256)(128)(2,1)} %gain_ref.1, bf16[1536,384]{1,0:T(8,128)(2,1)} %w_in.1, bf16[384,1536]{1,0:T(8,128)(2,1)} %w_out.1, ...), custom_call_target="tpu_custom_call" | custom-call | tf_op jit(solution)/shard_map/mlp_block/pallas_call | solution.py:740
  124.3 0.7 copy.15
  124.9 0.7 copy.16
  125.6 0.6 copy.17
  126.2 1.4 %copy.18 = f32[1536,384]{1,0:T(8,128)} copy(f32[1536,384]{1,0:T(8,128)S(1)} %get-tuple-element.18) | data formatting | bytes 4718592
  127.6 1.4 %copy.19 = f32[384,1536]{1,0:T(8,128)} copy(f32[384,1536]{1,0:T(8,128)S(1)} %get-tuple-element.19) | data formatting | bytes 4718592
